TPU v7x, 32 devices: a whole 2x2x4 slice. The times are simulated.
32 devices in a mesh: dp: 4 (over y, x), expert: 8 (over z, core).
Axes of the slice: x: 2, y: 2, z: 4, core: 2. Of those that a mesh axis runs over, the one named last changes fastest.
Arguments:
- tokens: bfloat16 [4096, 2048], P(('dp', 'expert')), may hold values from -6 to 6
- cotangent: bfloat16 [4096, 2048], P(('dp', 'expert')), may hold values from -6 to 6
- routes: int32 [4096, 8], P(('dp', 'expert')), may hold values from 0 to 63, all different within a row; in each aligned block of 128 rows (0 to 127, 128 to 255, ...) at most 18 rows name the same one
- probs: bfloat16 [4096, 8], P(('dp', 'expert')), may hold values from 0.019897461 to 0.29882812
- slot_expert: int32 [64], replicated, may hold values from 0 to 63, each once
- gate_w: bfloat16 [64, 2048, 384], P('expert', 'dp'), may hold values from -0.125 to 0.125
- up_w: bfloat16 [64, 2048, 384], P('expert', 'dp'), may hold values from -0.125 to 0.125
- down_w: bfloat16 [64, 384, 2048], P('expert', None, 'dp'), may hold values from -0.3125 to 0.3125
Outputs:
- grad_tokens: bfloat16 [4096, 2048], P(('dp', 'expert'))
- grad_probs: bfloat16 [4096, 8], P(('dp', 'expert'))
- grad_gate: float32 [64, 2048, 384], P('expert', 'dp')
- grad_up: float32 [64, 2048, 384], P('expert', 'dp')
- grad_down: float32 [64, 384, 2048], P('expert', None, 'dp')
Inputs may be any that keep to these rules, and one draw needn't show every extreme that they name: `routes`: in each aligned block of 128 rows (the tokens of one device) no expert is named by more than 18 rows, a bound that some block reaches; a row names 8 different experts. `slot_expert`: each expert stands in exactly one slot.
All inputs are finite; a program needn't handle non-finite values.
Results may differ from a plain program's by a relative error of at most 0.008.
Values may be sent and summed in bfloat16 or wider, within the bound.
No kernel may reach another device: no remote copies, remote signals or barrier semaphores. Data moves between devices by JAX's collectives and lax.ppermute only.
A program may use at most 192 MiB of HBM per device.

v0:
```python
import jax
import jax.numpy as jnp
from jax import lax
from jax.sharding import PartitionSpec as P

CAP = 18


def forward_part(got_x, w_gate, w_up):
    gate = jnp.einsum("sekd,edf->sekf", got_x, w_gate, preferred_element_type=jnp.float32)
    upval = jnp.einsum("sekd,edf->sekf", got_x, w_up, preferred_element_type=jnp.float32)
    sig = jax.nn.sigmoid(gate)
    act = gate * sig
    hidden = (act * upval).astype(jnp.bfloat16)
    return (gate, upval, sig, act, hidden)


def shards(tokens, cotangent, routes, probs, slot_expert, gate_w, up_w, down_w):
    n_exp = lax.axis_size("expert")
    local = gate_w.shape[0]
    tok_rows = tokens.shape[0]
    top = routes.shape[1]
    width = tokens.shape[1]
    count = local * n_exp
    rows_all = count * CAP
    flat = routes.reshape(-1)
    labels = jnp.arange(count, dtype=jnp.int32)
    match = slot_expert[None, :] == labels[:, None]
    slot_of = jnp.sum(jnp.where(match, labels[None, :], 0), axis=1)
    picked = flat[:, None] == labels[None, :]
    target = jnp.sum(jnp.where(picked, slot_of[None, :], 0), axis=1)
    hits = picked.astype(jnp.int32)
    position = jnp.sum((jnp.cumsum(hits, axis=0) - hits) * hits, axis=1)
    where_row = target * CAP + position
    placed = where_row[None, :] == jnp.arange(rows_all, dtype=jnp.int32)[:, None]
    token_map = jnp.any(placed.reshape(rows_all, tok_rows, top), axis=2).astype(jnp.bfloat16)
    send_x = jnp.dot(token_map, tokens, preferred_element_type=jnp.float32).astype(jnp.bfloat16)
    send_x = send_x.reshape(n_exp, local * CAP, width)
    send_dy = jnp.dot(token_map, cotangent, preferred_element_type=jnp.float32).astype(jnp.bfloat16)
    send_dy = send_dy.reshape(n_exp, local * CAP, width)
    zero_p = jnp.zeros((), jnp.bfloat16)
    send_p = jnp.sum(jnp.where(placed, probs.reshape(-1)[None, :], zero_p), axis=1).reshape(
        n_exp, local * CAP
    )
    w_gate, w_up, w_down = (
        lax.all_gather(gate_w, "dp", axis=1, tiled=True),
        lax.all_gather(up_w, "dp", axis=1, tiled=True),
        lax.all_gather(down_w, "dp", axis=2, tiled=True),
    )
    shape_rows = (n_exp, local, CAP, width)
    got_x = lax.all_to_all(send_x, "expert", split_axis=0, concat_axis=0, tiled=True).reshape(
        shape_rows
    )
    gate, upval, sig, act, hidden = forward_part(got_x, w_gate, w_up)
    got_dy, got_p = (
        lax.all_to_all(send_dy, "expert", split_axis=0, concat_axis=0, tiled=True),
        lax.all_to_all(send_p, "expert", split_axis=0, concat_axis=0, tiled=True),
    )
    got_dy = got_dy.reshape(shape_rows)
    weight = got_p.reshape(n_exp, local, CAP).astype(jnp.float32)[..., None]
    back = jnp.einsum("sekd,efd->sekf", got_dy, w_down, preferred_element_type=jnp.float32)
    dprob = jnp.sum(hidden.astype(jnp.float32) * back, axis=-1).astype(jnp.bfloat16)
    dh = weight * back
    d_gate = (dh * upval * sig * (1.0 + gate * (1.0 - sig))).astype(jnp.bfloat16)
    d_up = (dh * act).astype(jnp.bfloat16)
    dx_rows = (
        jnp.einsum("sekf,edf->sekd", d_gate, w_gate, preferred_element_type=jnp.float32)
        + jnp.einsum("sekf,edf->sekd", d_up, w_up, preferred_element_type=jnp.float32)
    ).astype(jnp.bfloat16)
    back_x, back_p = (
        lax.all_to_all(
            dx_rows.reshape(n_exp, local * CAP, width),
            "expert",
            split_axis=0,
            concat_axis=0,
            tiled=True,
        ),
        lax.all_to_all(
            dprob.reshape(n_exp, local * CAP), "expert", split_axis=0, concat_axis=0, tiled=True
        ),
    )
    wdy = (weight * got_dy.astype(jnp.float32)).astype(jnp.bfloat16)
    part_gate = jnp.einsum("sekd,sekf->edf", got_x, d_gate, preferred_element_type=jnp.float32)
    part_up = jnp.einsum("sekd,sekf->edf", got_x, d_up, preferred_element_type=jnp.float32)
    part_down = jnp.einsum("sekf,sekd->efd", hidden, wdy, preferred_element_type=jnp.float32)
    grad_gate, grad_up, grad_down = (
        lax.psum_scatter(part_gate, "dp", scatter_dimension=1, tiled=True),
        lax.psum_scatter(part_up, "dp", scatter_dimension=1, tiled=True),
        lax.psum_scatter(part_down, "dp", scatter_dimension=2, tiled=True),
    )
    returned_rows = back_x.reshape(rows_all, width)
    grad_tokens = lax.dot_general(
        token_map, returned_rows, (((0,), (0,)), ((), ())), preferred_element_type=jnp.float32
    ).astype(jnp.bfloat16)
    grad_probs = jnp.sum(jnp.where(placed, back_p.reshape(rows_all)[:, None], zero_p), axis=0)
    grad_probs = grad_probs.reshape(tok_rows, top)
    return (grad_tokens, grad_probs, grad_gate, grad_up, grad_down)


def solution(mesh):
    placed = (
        P(("dp", "expert"), None),
        P(("dp", "expert"), None),
        P(("dp", "expert"), None),
        P(("dp", "expert"), None),
        P(),
        P("expert", "dp", None),
        P("expert", "dp", None),
        P("expert", None, "dp"),
    )
    return jax.shard_map(
        shards,
        mesh=mesh,
        in_specs=placed,
        out_specs=(
            P(("dp", "expert"), None),
            P(("dp", "expert"), None),
            P("expert", "dp", None),
            P("expert", "dp", None),
            P("expert", None, "dp"),
        ),
        check_vma=False,
    )
```

profile of v0, /device:TPU:0, one launch (start us, length us, event | category | flops | bytes accessed | tf_op | source)
XLA Modules:
  0.0 1112.6 jit_solution(11889918747636957544)
XLA Ops:
  7.2 0.0 all-gather.6.cloned.1.call-start
  7.2 0.7 all-gather.6.cloned.1.call-update
  7.9 0.0 all-gather.8.cloned.1.call-start
  8.0 0.7 all-gather.8.cloned.1.call-update
  8.7 0.1 copy.88
  8.8 0.1 eq.58
  8.9 0.1 eq.65
  9.0 18.0 %reduce-window.6 = s32[64,8,128]{2,1,0:T(8,128)S(1)} reduce-window(s32[64,8,128]{2,1,0:T(8,128)S(1)} %fusion.36, s32[]{:T(128)} %constant.6.clone.1), window={size=1x1x128 pad=0_0x0_0x127_0}, to_apply=%region_2.3 | reduce-window | flops 8323072 | bytes 524292 | tf_op jit(solution)/shard_map/reduce-window
  27.0 0.1 slice.8
  27.2 0.1 copy.90
  27.3 0.1 copy.91
  27.4 0.1 select_reduce_fusion.1
  27.5 0.1 broadcast_add_fusion
  27.7 0.1 select_reduce_fusion
  27.8 0.1 add.28
  28.0 4.2 fusion.19
  32.2 3.6 convolution_convert_fusion
  35.8 6.5 all-to-all-start.2
  42.2 0.0 all-gather.4.cloned.1.call-start
  42.3 0.7 all-gather.4.cloned.1.call-update
  43.0 3.6 convolution_convert_fusion.1
  46.5 101.0 %all-to-all-done.2 = bf16[8,144,2048]{2,1,0:T(8,128)(2,1)} async-done(((bf16[8,144,2048]{2,1,0:T(8,128)(2,1)}), bf16[8,144,2048]{2,1,0:T(8,128)(2,1)}, u32[]{:S(2)}, u32[]{:S(2)}) %all-to-all-start.2) | async-done | bytes 4718624 | tf_op jit(solution)/shard_map/all_to_all | solution.py:51
  147.6 5.3 all-to-all-start.1
  152.8 7.1 copy.98
  159.9 97.6 %all-to-all-done.1 = bf16[8,144,2048]{2,1,0:T(8,128)(2,1)} async-done(((bf16[8,144,2048]{2,1,0:T(8,128)(2,1)}), bf16[8,144,2048]{2,1,0:T(8,128)(2,1)}, u32[]{:S(2)}, u32[]{:S(2)}) %all-to-all-start.1) | async-done | bytes 4718624 | tf_op jit(solution)/shard_map/all_to_all | solution.py:56
  257.5 7.1 copy.96
  264.6 13.0 %fusion.8 = f32[8,8,18,384]{3,2,1,0:T(8,128)S(1)} fusion(bf16[8,2048,384]{2,1,0:T(8,128)(2,1)} %all-gather.6.cloned.1.call-done, bf16[8,8,18,2048]{3,0,2,1:T(8,128)(2,1)} %bitcast.118), kind=kOutput, calls=%fused_computation.8 | convolution fusion | flops 1811939328 | bytes 19070976 | tf_op jit(solution)/shard_map/sekd,edf->sekf/dot_general | solution.py:11
  277.6 0.0 all-gather.8.cloned.1.call-done
  277.7 13.6 %fusion.2 = f32[8,8,18,384]{3,2,1,0:T(8,128)} fusion(bf16[8,2048,384]{2,1,0:T(8,128)(2,1)} %all-gather.8.cloned.1.call-done, bf16[8,8,18,2048]{3,0,2,1:T(8,128)(2,1)} %bitcast.119), kind=kOutput, calls=%fused_computation.2 | convolution fusion | flops 1811939328 | bytes 19070976 | tf_op jit(solution)/shard_map/sekd,edf->sekf/dot_general | solution.py:10
  291.3 92.5 %all-gather.4.cloned.1.call-done = bf16[8,384,2048]{2,1,0:T(8,128)(2,1)} async-done(((bf16[8,384,512]{2,1,0:T(8,128)(2,1)}), bf16[8,384,2048]{2,1,0:T(8,128)(2,1)}) %all-gather.4.cloned.1.call-update) | async-done | bytes 12582928 | tf_op jit(solution)/shard_map/all_gather | solution.py:48
  383.8 11.0 fusion.30
  394.8 0.7 convert_element_type.87
  395.5 4.6 all-to-all-start.4
  400.1 0.0 reduce-scatter.4.cloned.1.call-start
  400.2 0.1 copy.93
  400.3 0.1 broadcast_in_dim.62
  400.4 5.3 all-to-all-done.4
  405.8 0.1 broadcast_in_dim.65
  405.9 1.7 fusion.21
  407.5 0.1 all_to_all.25
  407.6 8.2 all_to_all.31
  415.8 0.1 reshape.109
  415.9 3.7 multiply_convert_fusion.1
  419.6 15.3 %convolution_bitcast_fusion.2 = f32[8,2048,384]{2,1,0:T(8,128)} fusion(bf16[8,8,18,2048]{3,0,2,1:T(8,128)(2,1)} %bitcast.120, bf16[8,8,18,384]{3,2,0,1:T(8,128)(2,1)S(1)} %get-tuple-element.37), kind=kOutput, calls=%fused_computation.14 | convolution fusion | flops 1811939328 | bytes 30769152 | tf_op jit(solution)/shard_map/sekd,sekf->edf/dot_general | solution.py:83
  434.9 0.0 reduce-scatter.4.cloned.1.call-update
  434.9 0.0 reduce-scatter.6.cloned.1.call-start
  434.9 15.8 %convolution_bitcast_fusion.1 = f32[8,2048,384]{2,1,0:T(8,128)} fusion(bf16[8,8,18,2048]{3,0,2,1:T(8,128)(2,1)} %bitcast.121, bf16[8,8,18,384]{3,2,0,1:T(8,128)(2,1)S(1)} %get-tuple-element.36), kind=kOutput, calls=%fused_computation.13 | convolution fusion | flops 1811939328 | bytes 30769152 | tf_op jit(solution)/shard_map/sekd,sekf->edf/dot_general | solution.py:84
  450.8 0.0 reduce-scatter.8.cloned.1.call-start
  450.8 0.7 copy-done.7
  451.5 0.1 copy.107
  451.6 3.3 multiply_convert_fusion
  454.9 11.5 %convolution_bitcast_fusion = f32[8,384,2048]{2,1,0:T(8,128)} fusion(bf16[8,8,18,384]{3,2,0,1:T(8,128)(2,1)S(1)} %copy-done.12, bf16[8,8,18,2048]{3,0,2,1:T(8,128)(2,1)S(1)} %multiply_convert_fusion), kind=kOutput, calls=%fused_computation.12 | convolution fusion | flops 1811939328 | bytes 30769152 | tf_op jit(solution)/shard_map/sekf,sekd->efd/dot_general | solution.py:85
  466.4 15.1 %fusion = f32[8,8,18,2048]{3,2,1,0:T(8,128)} fusion(bf16[8,8,18,384]{3,2,0,1:T(8,128)(2,1)S(1)} %get-tuple-element.37, bf16[8,2048,384]{2,1,0:T(8,128)(2,1)} %all-gather.8.cloned.1.call-done), kind=kOutput, calls=%fused_computation | convolution fusion | flops 1811939328 | bytes 22904832 | tf_op jit(solution)/shard_map/sekf,edf->sekd/dot_general | solution.py:67
  481.5 14.0 %fusion.12 = bf16[8,8,18,2048]{3,2,0,1:T(8,128)(2,1)} fusion(f32[8,8,18,2048]{3,2,1,0:T(8,128)} %fusion, bf16[8,8,18,384]{3,2,0,1:T(8,128)(2,1)S(1)} %get-tuple-element.36, bf16[8,2048,384]{2,1,0:T(8,128)(2,1)} %all-gather.6.cloned.1.call-done), kind=kOutput, calls=%fused_computation.19 | convolution fusion | flops 1816657920 | bytes 27623424 | tf_op jit(solution)/shard_map/sekf,edf->sekd/dot_general | solution.py:68
  495.5 5.9 copy.101
  501.4 4.7 copy.102
  506.1 4.8 all-to-all-start.3
  510.9 0.1 reshape.108
  511.0 0.7 copy.109
  511.7 104.5 %all-to-all-done.3 = bf16[8,144,2048]{2,1,0:T(8,128)(2,1)} async-done(((bf16[8,144,2048]{2,1,0:T(8,128)(2,1)}), bf16[8,144,2048]{2,1,0:T(8,128)(2,1)}, u32[]{:S(2)}, u32[]{:S(2)}) %all-to-all-start.3) | async-done | bytes 4718624 | tf_op jit(solution)/shard_map/all_to_all | solution.py:71
  616.2 4.2 convolution_convert_fusion.2
  620.3 33.8 %reduce-scatter.4.cloned.1.call-done = f32[8,512,384]{2,1,0:T(8,128)} async-done(((f32[8,2048,384]{2,1,0:T(8,128)}), f32[8,512,384]{2,1,0:T(8,128)}) %reduce-scatter.4.cloned.1.call-update) | async-done | bytes 6291472 | tf_op jit(solution)/shard_map/reduce_scatter | solution.py:87
  654.2 225.7 %reduce-scatter.6.cloned.1.call-done = f32[8,512,384]{2,1,0:T(8,128)} async-done(((f32[8,2048,384]{2,1,0:T(8,128)}), f32[8,512,384]{2,1,0:T(8,128)}) %reduce-scatter.6.cloned.1.call-update) | async-done | bytes 6291472 | tf_op jit(solution)/shard_map/reduce_scatter | solution.py:88
  879.9 225.4 %reduce-scatter.8.cloned.1.call-done = f32[8,384,512]{2,1,0:T(8,128)} async-done(((f32[8,384,2048]{2,1,0:T(8,128)}), f32[8,384,512]{2,1,0:T(8,128)}) %reduce-scatter.8.cloned.1.call-update) | async-done | bytes 6291472 | tf_op jit(solution)/shard_map/reduce_scatter | solution.py:89
  (37 shorter events, 0.3 us)
Async XLA Ops:
  7.2 25.0 %copy-start = (bf16[128,2048]{1,0:T(8,128)(2,1)S(1)}, bf16[128,2048]{1,0:T(8,128)(2,1)}, u32[]{:S(2)}) copy-start(bf16[128,2048]{1,0:T(8,128)(2,1)} %param.8) | copy-start | bytes 1572868
  7.2 1.5 copy-start.8
  7.2 20.2 %copy-start.11 = (s32[64]{0:T(128)S(1)}, s32[64]{0:T(128)}, u32[]{:S(2)}) copy-start(s32[64]{0:T(128)} %param.12) | copy-start | bytes 772
  7.2 257.4 %all-gather.6.cloned.1.call-start = ((), (), s32[]{:S(2)}) async-start(), calls=%async_computation.9 | async-start | bytes 15728640 | tf_op jit(solution)/shard_map/all_gather | solution.py:47
  7.9 269.7 %all-gather.8.cloned.1.call-start = ((), (), s32[]{:S(2)}) async-start(), calls=%async_computation.10 | async-start | bytes 15728640 | tf_op jit(solution)/shard_map/all_gather | solution.py:46
  32.2 10.8 copy-start.2
  35.7 7.2 copy-start.5
  35.8 111.8 %all-to-all-start.2 = ((bf16[8,144,2048]{2,1,0:T(8,128)(2,1)}), bf16[8,144,2048]{2,1,0:T(8,128)(2,1)}, u32[]{:S(2)}, u32[]{:S(2)}) async-start(bf16[8,144,2048]{2,1,0:T(8,128)(2,1)} %bitcast.113), calls=%async_computation.2 | async-start | bytes 9437184 | tf_op jit(solution)/shard_map/all_to_all | solution.py:51
  42.2 341.6 %all-gather.4.cloned.1.call-start = ((), (), s32[]{:S(2)}) async-start(), calls=%async_computation.8 | async-start | bytes 15728640 | tf_op jit(solution)/shard_map/all_gather | solution.py:48
  147.6 110.0 %all-to-all-start.1 = ((bf16[8,144,2048]{2,1,0:T(8,128)(2,1)}), bf16[8,144,2048]{2,1,0:T(8,128)(2,1)}, u32[]{:S(2)}, u32[]{:S(2)}) async-start(bf16[8,144,2048]{2,1,0:T(8,128)(2,1)} %bitcast.114), calls=%async_computation.1 | async-start | bytes 9437184 | tf_op jit(solution)/shard_map/all_to_all | solution.py:56
  277.6 106.2 %copy-start.4 = (f32[8,8,18,384]{3,2,1,0:T(8,128)}, f32[8,8,18,384]{3,2,1,0:T(8,128)S(1)}, u32[]{:S(2)}) copy-start(f32[8,8,18,384]{3,2,1,0:T(8,128)S(1)} %fusion.8) | copy-start | bytes 5308420
  383.8 16.4 %copy-start.9 = (bf16[128,8]{0,1:T(8,128)(2,1)S(1)}, bf16[128,8]{0,1:T(8,128)(2,1)}, u32[]{:S(2)}) copy-start(bf16[128,8]{0,1:T(8,128)(2,1)} %param.11) | copy-start | bytes 6148
  395.5 10.2 all-to-all-start.4
  400.1 254.1 %reduce-scatter.4.cloned.1.call-start = ((), (), s32[]{:S(2)}) async-start(), calls=%async_computation.11 | async-start | bytes 31457280 | tf_op jit(solution)/shard_map/reduce_scatter | solution.py:87
  415.9 3.7 copy-start.6
  434.9 445.0 %reduce-scatter.6.cloned.1.call-start = ((), (), s32[]{:S(2)}) async-start(), calls=%async_computation.12 | async-start | bytes 31457280 | tf_op jit(solution)/shard_map/reduce_scatter | solution.py:88
  450.7 0.8 copy-start.7
  450.8 654.5 %reduce-scatter.8.cloned.1.call-start = ((), (), s32[]{:S(2)}) async-start(), calls=%async_computation.13 | async-start | bytes 31457280 | tf_op jit(solution)/shard_map/reduce_scatter | solution.py:89
  451.6 3.3 copy-start.12
  506.1 4.8 copy-start.10
  506.1 110.0 %copy-start.3 = (pred[1152,128]{1,0:T(8,128)(4,1)S(1)}, pred[1152,128]{1,0:T(8,128)(4,1)}, u32[]{:S(2)}) copy-start(pred[1152,128]{1,0:T(8,128)(4,1)} %copy-done.2) | copy-start | bytes 442372
  506.1 110.0 %all-to-all-start.3 = ((bf16[8,144,2048]{2,1,0:T(8,128)(2,1)}), bf16[8,144,2048]{2,1,0:T(8,128)(2,1)}, u32[]{:S(2)}, u32[]{:S(2)}) async-start(bf16[8,144,2048]{2,1,0:T(8,128)(2,1)} %copy.102), calls=%async_computation.3 | async-start | bytes 9437184 | tf_op jit(solution)/shard_map/all_to_all | solution.py:71
  510.9 594.4 %copy-start.1 = (bf16[128,2048]{1,0:T(8,128)(2,1)S(1)}, bf16[128,2048]{1,0:T(8,128)(2,1)}, u32[]{:S(2)}) copy-start(bf16[128,2048]{1,0:T(8,128)(2,1)} %param.8) | copy-start | bytes 1572868
Sparse Core Ops, SparseCore 0:
  9.9 125.2 all-gather.5
  137.0 122.5 all-gather.7
  261.4 122.3 all-gather.3
  435.0 219.1 reduce-scatter.3
  658.0 221.8 reduce-scatter.5
  883.4 221.8 reduce-scatter.7
where the time goes:
time: 1120 us; the launch traced here: 1110 us
  waiting for transfers between devices  888 us (79%)
  matrix products  121 us (11%)
  other arithmetic  31.3 us (3%)
  local copies, waits for them, and re-layouts  28.4 us (3%)
  starting transfers between devices  21.3 us (2%)
  between operations  14.9 us (1%)
    reduce_scatter x1, waiting for transfers between devices, shards(): lax.psum_scatter(part_up, 'dp', scatter_dimension=1, tiled=True)  226 us
    reduce_scatter x1, waiting for transfers between devices, shards(): lax.psum_scatter(part_down, 'dp', scatter_dimension=2, tiled=True)  225 us
    all_to_all x1, waiting for transfers between devices, shards(): lax.all_to_all(dx_rows.reshape(n_exp, local * CAP, width), 'expert', spli...  104 us
    all_to_all x1, waiting for transfers between devices, shards(): lax.all_to_all(send_x, 'expert', split_axis=0, concat_axis=0, tiled=True)  101 us
    all_to_all x1, waiting for transfers between devices, shards(): lax.all_to_all(send_dy, 'expert', split_axis=0, concat_axis=0, tiled=True)  97.6 us
    all_gather x1, waiting for transfers between devices, shards(): lax.all_gather(down_w, 'dp', axis=2, tiled=True)  92.5 us
    reduce_scatter x1, waiting for transfers between devices, shards(): lax.psum_scatter(part_gate, 'dp', scatter_dimension=1, tiled=True)  33.8 us
  transfers between devices with their start and end apart: 10, of which 8 were waited for; matrix products, arithmetic and copies ran while one was open for 13% of the time, Pallas kernels for 0%

commit v1 on v0

--- a/solution.py
+++ b/solution.py
@@ -1,9 +1,447 @@
+import functools
+
 import jax
 import jax.numpy as jnp
 from jax import lax
+from jax.experimental import pallas as pl
+from jax.experimental.pallas import tpu as pltpu
 from jax.sharding import PartitionSpec as P
 
 CAP = 18
+F32 = jnp.float32
+BF16 = jnp.bfloat16
+VMEM_LIMIT = 48 * 1024 * 1024
+NT = (((1,), (1,)), ((), ()))
+TN = (((0,), (0,)), ((), ()))
+NN = (((1,), (0,)), ((), ()))
+
+
+def mm(a, b, dims=NN):
+    return lax.dot_general(a, b, dims, preferred_element_type=F32)
+
+
+def params():
+    return pltpu.CompilerParams(vmem_limit_bytes=VMEM_LIMIT)
+
+
+def cost(flops, nbytes):
+    return pl.CostEstimate(flops=int(flops), bytes_accessed=int(nbytes), transcendentals=0)
+
+
+def payload_kernel(info, tok, cot, routes, probs, experts, *outs):
+    n = info[8]
+    rows, width = tok.shape
+    wide = width // len(outs)
+    lanes = experts.shape[1]
+    lane = lax.broadcasted_iota(jnp.int32, (rows, lanes), 1)
+    hit = jnp.zeros((rows, lanes), F32)
+    val = jnp.zeros((rows, lanes), F32)
+    want = experts[...]
+    rt = routes[...]
+    pr = probs[...].astype(F32)
+    for k in range(routes.shape[1]):
+        eq = rt[:, k : k + 1] == want
+        hit = jnp.where(eq, 1.0, hit)
+        val = jnp.where(eq, pr[:, k : k + 1], val)
+    before = (
+        lax.broadcasted_iota(jnp.int32, (rows, rows), 1)
+        < lax.broadcasted_iota(jnp.int32, (rows, rows), 0)
+    ).astype(F32).astype(BF16)
+    pos = mm(before, hit.astype(BF16))
+    pos = jnp.where(hit > 0.5, pos, -1.0)
+    meta = jnp.where(lane < lanes // 2, pos, val).astype(BF16)
+    for o, out in enumerate(outs):
+        at = pl.multiple_of((n ^ o) * wide, wide)
+        out[:, :wide] = tok[:, pl.ds(at, wide)]
+        out[:, wide : 2 * wide] = cot[:, pl.ds(at, wide)]
+        out[:, 2 * wide :] = meta
+
+
+def payload(info, tokens, cotangent, routes, probs, slot_expert, n_dp):
+    rows, width = tokens.shape
+    wide = width // n_dp
+    twice = jnp.concatenate([slot_expert, slot_expert])[None, :]
+    cols = 2 * wide + twice.shape[1]
+    return pl.pallas_call(
+        payload_kernel,
+        in_specs=[pl.BlockSpec(memory_space=pltpu.SMEM)] + [pl.BlockSpec(memory_space=pltpu.VMEM)] * 5,
+        out_specs=[pl.BlockSpec(memory_space=pltpu.VMEM)] * n_dp,
+        out_shape=[jax.ShapeDtypeStruct((rows, cols), BF16)] * n_dp,
+        compiler_params=params(),
+        name="payload",
+    )(info, tokens, cotangent, routes, probs, twice)
+
+
+def partial_kernel(n_dp, tok, base, keep, *refs):
+    info, own, sib, gate, up, down = refs[:6]
+    refs = refs[6:]
+    xs, dys, dest_out = refs[:3]
+    scr = refs[-1]
+    g = pl.program_id(0)
+    n, first, core = info[8], info[9], info[10]
+    wide = xs.shape[-1]
+    lanes = own.shape[1] - 2 * wide
+    half = lanes // 2
+
+    @pl.when(g == 0)
+    def _():
+        for c, src in enumerate((own, sib)):
+            for o in range(n_dp):
+                table = src[o * tok : (o + 1) * tok, 2 * wide :].astype(F32)
+                scr[c * n_dp + o] = table.T
+
+    row = first + info[base + g]
+    rows = xs.shape[2]
+    dests = []
+    weights = []
+    for c in range(2):
+        for o in range(n_dp):
+            pos = scr[c * n_dp + o, pl.ds(row, 1), :]
+            off = (((n ^ o) * 2 + (core ^ c)) * CAP).astype(F32)
+            dests.append(jnp.where(pos < 0, -1.0, pos + off))
+            if keep:
+                weights.append(scr[c * n_dp + o, pl.ds(half + row, 1), :])
+    dest = jnp.concatenate(dests, axis=1).astype(jnp.int32)
+    dest_out[0] = dest
+    hot = (lax.broadcasted_iota(jnp.int32, (rows, dest.shape[1]), 0) == dest).astype(F32)
+    pick = hot.astype(BF16)
+    m = n_dp * tok
+    got = mm(pick[:, :m], own[:, : 2 * wide]) + mm(pick[:, m:], sib[:, : 2 * wide])
+    got = got.astype(BF16)
+    x, dy = got[:, :wide], got[:, wide:]
+    xs[0, 0] = x
+    dys[0, 0] = dy
+    gg = mm(x, gate[0])
+    uu = mm(x, up[0])
+    rr = mm(dy, down[0], NT)
+    f = gg.shape[1]
+
+    def put(out, lead):
+        out[lead, :, :f] = gg.astype(out.dtype)
+        out[lead, :, f : 2 * f] = uu.astype(out.dtype)
+        out[lead, :, 2 * f :] = rr.astype(out.dtype)
+
+    if keep:
+        put(refs[3], 0)
+        prob_out = refs[4]
+
+        @pl.when(g >= 2)
+        def _():
+            p = jnp.sum(hot * jnp.concatenate(weights, axis=1), axis=1, keepdims=True)
+            prob_out[0] = jnp.broadcast_to(p, prob_out.shape[1:])
+    else:
+        for q in range(4):
+
+            @pl.when(g == q)
+            def _():
+                put(refs[3 + q], 0)
+
+
+def partials(info, own, sib, gate_w, up_w, down_w, bufs, chunk, n_chunk, keep, n_dp, tok):
+    local, wide, f = gate_w.shape
+    rows = 2 * n_dp * CAP
+    base = 4 if keep else 0
+    total = 2 * n_dp * tok
+    at = lambda g, s: (s[base + g], 0, 0)
+    buf_at = lambda g, s: (s[base + g], chunk, 0, 0)
+    whole = lambda g, s: (0, 0)
+    in_specs = [
+        pl.BlockSpec(own.shape, whole),
+        pl.BlockSpec(sib.shape, whole),
+        pl.BlockSpec((1, wide, f), at),
+        pl.BlockSpec((1, wide, f), at),
+        pl.BlockSpec((1, f, wide), at),
+    ]
+    args = [info, own, sib, gate_w, up_w, down_w]
+    out_shape = [jax.ShapeDtypeStruct((local, n_chunk, rows, wide), BF16)] * 2
+    out_shape += [jax.ShapeDtypeStruct((4, 1, total), jnp.int32)]
+    out_specs = [pl.BlockSpec((1, 1, rows, wide), buf_at)] * 2
+    out_specs += [pl.BlockSpec((1, 1, total), lambda g, s: (g, 0, 0))]
+    aliases = {}
+    if bufs is not None:
+        in_specs += [pl.BlockSpec(memory_space=pl.ANY)] * 2
+        args += list(bufs)
+        aliases = {6: 0, 7: 1}
+    if keep:
+        out_shape += [jax.ShapeDtypeStruct((4, rows, 3 * f), F32), jax.ShapeDtypeStruct((2, rows, 128), F32)]
+        out_specs += [
+            pl.BlockSpec((1, rows, 3 * f), lambda g, s: (g, 0, 0)),
+            pl.BlockSpec((1, rows, 128), lambda g, s: (jnp.maximum(g - 2, 0), 0, 0)),
+        ]
+    else:
+        out_shape += [jax.ShapeDtypeStruct((1, rows, 3 * f), BF16)] * 4
+        out_specs += [pl.BlockSpec((1, rows, 3 * f), lambda g, s: (0, 0, 0))] * 4
+
+    def kernel(*refs):
+        if bufs is not None:
+            refs = refs[:6] + refs[8:]
+        partial_kernel(n_dp, tok, base, keep, *refs)
+
+    return pl.pallas_call(
+        kernel,
+        grid_spec=pltpu.PrefetchScalarGridSpec(
+            num_scalar_prefetch=1,
+            grid=(4,),
+            in_specs=in_specs,
+            out_specs=out_specs,
+            scratch_shapes=[pltpu.VMEM((2 * n_dp, own.shape[1] - 2 * wide, tok), F32)],
+        ),
+        out_shape=out_shape,
+        input_output_aliases=aliases,
+        compiler_params=params(),
+        cost_estimate=cost(8 * rows * (total * 2 * wide + wide * 3 * f), 8e6),
+        name="partials_keep" if keep else "partials_send",
+    )(*args)
+
+
+def inner_kernel(n_dp, tok, info, keep, raw_a, sum_a, raw_b, sum_b, prob, dest, *refs):
+    act, table = refs[-2:]
+    n, core = info[8], info[10]
+    f = act.shape[1] // 3
+    rows = keep.shape[1]
+    for h, (raw, summed) in enumerate(((raw_a, sum_a), (raw_b, sum_b))):
+        t = keep[2 + h] + raw[0].astype(F32) + summed[0].astype(F32)
+        g, u, r = t[:, :f], t[:, f : 2 * f], t[:, 2 * f :]
+        sg = jax.nn.sigmoid(g)
+        silu = g * sg
+        hid = silu * u
+        p = prob[h][:, :1]
+        pr = p * r
+        hb = hid.astype(BF16).astype(F32)
+        dprob = jnp.sum(hb * r, axis=1, keepdims=True)
+        at = slice(h * rows, (h + 1) * rows)
+        act[at, :f] = (pr * u * sg * (1.0 + g * (1.0 - sg))).astype(BF16)
+        act[at, f : 2 * f] = (pr * silu).astype(BF16)
+        act[at, 2 * f :] = (p * hid).astype(BF16)
+        want = dest[2 + h]
+        eq = lax.broadcasted_iota(jnp.int32, (rows, want.shape[1]), 0) == want
+        line = jnp.sum(jnp.where(eq, dprob, 0.0), axis=0, keepdims=True)
+        for c in range(2):
+            for o in range(n_dp):
+                k = c * n_dp + o
+                table[n ^ o, 0, core ^ c, pl.ds(h, 1), :] = line[:, k * tok : (k + 1) * tok]
+
+
+def inner(info, keep, raw_a, sum_a, raw_b, sum_b, prob, dest, table, chunk, n_chunk, n_dp, tok):
+    rows, f3 = keep.shape[1:]
+    args = [info, keep, raw_a, sum_a, raw_b, sum_b, prob, dest]
+    full = lambda a: pl.BlockSpec(a.shape, lambda g, s: (0,) * a.ndim)
+    in_specs = [full(a) for a in args[1:]]
+    aliases = {}
+    if table is not None:
+        args.append(table)
+        in_specs.append(pl.BlockSpec(memory_space=pl.ANY))
+        aliases = {8: 1}
+    return pl.pallas_call(
+        functools.partial(inner_kernel, n_dp, tok),
+        grid_spec=pltpu.PrefetchScalarGridSpec(
+            num_scalar_prefetch=1,
+            grid=(1,),
+            in_specs=in_specs,
+            out_specs=[
+                pl.BlockSpec((2 * rows, f3), lambda g, s: (0, 0)),
+                pl.BlockSpec((n_dp, 1, 2, 2, tok), lambda g, s: (0, s[11 + chunk], 0, 0, 0)),
+            ],
+        ),
+        out_shape=[
+            jax.ShapeDtypeStruct((2 * rows, f3), BF16),
+            jax.ShapeDtypeStruct((n_dp, n_chunk, 2, 2, tok), F32),
+        ],
+        input_output_aliases=aliases,
+        compiler_params=params(),
+        cost_estimate=cost(2 * rows * f3 * 20, 6e6),
+        name="inner",
+    )(*args)
+
+
+def dx_kernel(info, own, from_x, from_y, far_a, far_b, dest_s, dest_k, gate, up, *refs):
+    acts, out_own, out_sib, act_s, hot_s, dx_s = refs[-6:]
+    g = pl.program_id(0)
+    rows = far_a.shape[0]
+    f = gate.shape[2]
+
+    @pl.when(g == 0)
+    def _():
+        act_s[0] = far_a[...]
+        act_s[1] = far_b[...]
+        act_s[2] = from_x[:rows]
+        act_s[3] = from_y[rows:]
+        act_s[4] = from_y[:rows]
+        act_s[5] = from_x[rows:]
+        act_s[6] = own[:rows]
+        act_s[7] = own[rows:]
+
+    a = act_s[g]
+    acts[0, 0] = a
+    back = mm(a[:, :f], gate[0], NT) + mm(a[:, f : 2 * f], up[0], NT)
+    at = pl.ds(pl.multiple_of(g * rows, rows), rows)
+    dx_s[at, :] = back.astype(BF16)
+    want = jnp.where(g < 4, dest_s[jnp.minimum(g, 3)], dest_k[jnp.maximum(g - 4, 0)])
+    hot = lax.broadcasted_iota(jnp.int32, (rows, want.shape[1]), 0) == want
+    hot_s[at, :] = hot.astype(F32).astype(BF16)
+
+    @pl.when(g == 7)
+    def _():
+        m = out_own.shape[0]
+        out_sib[...] = mm(hot_s[:, m:], dx_s[...], TN).astype(out_sib.dtype)
+        out_own[...] = mm(hot_s[:, :m], dx_s[...], TN).astype(out_own.dtype)
+
+
+def dx_chunk(info, own, from_x, from_y, far_a, far_b, dest_s, dest_k, gate_w, up_w, acts, chunk, n_chunk):
+    local, wide, f = gate_w.shape
+    rows, f3 = far_a.shape
+    total = dest_s.shape[-1]
+    args = [info, own, from_x, from_y, far_a, far_b, dest_s, dest_k, gate_w, up_w]
+    full = lambda a: pl.BlockSpec(a.shape, lambda g, s: (0,) * a.ndim)
+    at = lambda g, s: (s[g], 0, 0)
+    in_specs = [full(a) for a in args[1:8]] + [pl.BlockSpec((1, wide, f), at)] * 2
+    aliases = {}
+    if acts is not None:
+        args.append(acts)
+        in_specs.append(pl.BlockSpec(memory_space=pl.ANY))
+        aliases = {10: 0}
+    half = pl.BlockSpec((total // 2, wide), lambda g, s: (0, 0))
+    return pl.pallas_call(
+        dx_kernel,
+        grid_spec=pltpu.PrefetchScalarGridSpec(
+            num_scalar_prefetch=1,
+            grid=(8,),
+            in_specs=in_specs,
+            out_specs=[pl.BlockSpec((1, 1, rows, f3), lambda g, s: (s[g], chunk, 0, 0)), half, half],
+            scratch_shapes=[
+                pltpu.VMEM((8, rows, f3), BF16),
+                pltpu.VMEM((8 * rows, total), BF16),
+                pltpu.VMEM((8 * rows, wide), BF16),
+            ],
+        ),
+        out_shape=[
+            jax.ShapeDtypeStruct((local, n_chunk, rows, f3), BF16),
+            jax.ShapeDtypeStruct((total // 2, wide), F32),
+            jax.ShapeDtypeStruct((total // 2, wide), BF16),
+        ],
+        input_output_aliases=aliases,
+        compiler_params=params(),
+        cost_estimate=cost(2 * 8 * rows * (2 * f * wide + total * wide), 12e6),
+        name="dx",
+    )(*args)
+
+
+def grads_kernel(xs, dys, acts, out_gate, out_up, out_down):
+    f = out_gate.shape[2]
+    flat = lambda ref: ref[0].reshape(-1, ref.shape[-1])
+    x, dy, a = flat(xs), flat(dys), flat(acts)
+    both = mm(x, a[:, : 2 * f], TN)
+    out_gate[0] = both[:, :f]
+    out_up[0] = both[:, f:]
+    out_down[0] = mm(a[:, 2 * f :], dy, TN)
+
+
+def grads(xs, dys, acts):
+    local, n_chunk, rows, wide = xs.shape
+    f = acts.shape[-1] // 3
+    spec = lambda a: pl.BlockSpec((1,) + a.shape[1:], lambda g: (g, 0, 0, 0))
+    shapes = [(local, wide, f), (local, wide, f), (local, f, wide)]
+    return pl.pallas_call(
+        grads_kernel,
+        grid=(local,),
+        in_specs=[spec(xs), spec(dys), spec(acts)],
+        out_specs=[pl.BlockSpec((1,) + s[1:], lambda g: (g, 0, 0)) for s in shapes],
+        out_shape=[jax.ShapeDtypeStruct(s, F32) for s in shapes],
+        compiler_params=params(),
+        cost_estimate=cost(6 * local * n_chunk * rows * wide * f, 30e6),
+        name="grads",
+    )(xs, dys, acts)
+
+
+def join_kernel(info, *refs):
+    out = refs[-1]
+    wide = refs[0].shape[1]
+    for o, piece in enumerate(refs[:-1]):
+        out[:, pl.ds(pl.multiple_of((info[8] ^ o) * wide, wide), wide)] = piece[...]
+
+
+def join(info, pieces):
+    rows, wide = pieces[0].shape
+    return pl.pallas_call(
+        join_kernel,
+        in_specs=[pl.BlockSpec(memory_space=pltpu.SMEM)] + [pl.BlockSpec(memory_space=pltpu.VMEM)] * len(pieces),
+        out_specs=pl.BlockSpec(memory_space=pltpu.VMEM),
+        out_shape=jax.ShapeDtypeStruct((rows, wide * len(pieces)), BF16),
+        compiler_params=params(),
+        name="join",
+    )(info, *pieces)
+
+
+def shards_rows(tokens, cotangent, routes, probs, slot_expert, gate_w, up_w, down_w):
+    n_dp, n_exp = lax.axis_size("dp"), lax.axis_size("expert")
+    local = gate_w.shape[0]
+    tok = tokens.shape[0]
+    n_chunk = n_exp // 2
+    rows = 2 * n_dp * CAP
+    n, e = lax.axis_index("dp"), lax.axis_index("expert")
+    order = [3, 7, 1, 6, 2, 5, 0, 4]
+    info = jnp.stack(
+        [2 * (n ^ (k % 4)) + k // 4 for k in order]
+        + [n, e * local, e % 2]
+        + [(e // 2 - j) % n_chunk for j in range(n_chunk)]
+    ).astype(jnp.int32)
+
+    def swap(a, o):
+        return lax.ppermute(a, "dp", [(k, k ^ o) for k in range(n_dp)])
+
+    def sibling(a):
+        return lax.ppermute(a, "expert", [(k, k ^ 1) for k in range(n_exp)])
+
+    def plane(a):
+        return lax.ppermute(a, "expert", [(k, (k + 2) % n_exp) for k in range(n_exp)])
+
+    sends = payload(info, tokens, cotangent, routes, probs, slot_expert, n_dp)
+    own = jnp.concatenate([sends[0]] + [swap(sends[o], o) for o in range(1, n_dp)], axis=0)
+
+    xy_bufs, acts, table = None, None, None
+    home, ring = None, None
+    for j in range(n_chunk):
+        sib = sibling(own)
+        xs, dys, dest_s, a3, b3, a1, b2 = partials(
+            info, own, sib, gate_w, up_w, down_w, xy_bufs, j, n_chunk, False, n_dp, tok
+        )
+        got_a3, got_b3 = swap(a3, 1), swap(b3, 2)
+        raw_a, raw_b = swap(a1, 1), swap(b2, 2)
+        xs, dys, dest_k, keep, prob = partials(
+            info, own, sib, gate_w, up_w, down_w, (xs, dys), j, n_chunk, True, n_dp, tok
+        )
+        xy_bufs = (xs, dys)
+        if j + 1 < n_chunk:
+            own = plane(own)
+        sum_a = swap((keep[0:1] + got_a3.astype(F32)).astype(BF16), 2)
+        sum_b = swap((keep[1:2] + got_b3.astype(F32)).astype(BF16), 1)
+        act, table = inner(
+            info, keep, raw_a, sum_a, raw_b, sum_b, prob, dest_k, table, j, n_chunk, n_dp, tok
+        )
+        from_x, from_y = swap(act, 1), swap(act, 2)
+        far_a, far_b = swap(from_y[:rows], 1), swap(from_x[rows:], 2)
+        acts, dx_own, dx_sib = dx_chunk(
+            info, act, from_x, from_y, far_a, far_b, dest_s, dest_k, gate_w, up_w, acts, j, n_chunk
+        )
+        dx = dx_own + sibling(dx_sib).astype(F32)
+        if j == 0:
+            home = dx
+        else:
+            if ring is not None:
+                dx = dx + ring.astype(F32)
+            ring = plane(dx.astype(BF16))
+    grad_gate, grad_up, grad_down = grads(xs, dys, acts)
+    if ring is not None:
+        home = home + ring.astype(F32)
+    home = home.astype(BF16)
+    pieces = [home[o * tok : (o + 1) * tok] for o in range(n_dp)]
+    grad_tokens = join(info, [pieces[0]] + [swap(pieces[o], o) for o in range(1, n_dp)])
+    flat = table.astype(BF16).reshape(n_dp * n_exp, 2, tok)
+    flat = lax.all_to_all(flat, ("dp", "expert"), 0, 0, tiled=True)
+    by_slot = flat.reshape(n_dp, n_exp, 2, tok).transpose(1, 0, 2, 3).reshape(n_exp * local, tok)
+    match = routes[:, :, None] == slot_expert[None, None, :]
+    grad_probs = jnp.sum(jnp.where(match, by_slot.T[:, None, :], jnp.zeros((), BF16)), axis=2)
+    return (grad_tokens, grad_probs, grad_gate, grad_up, grad_down)
 
 
 def forward_part(got_x, w_gate, w_up):
@@ -15,7 +453,7 @@
     return (gate, upval, sig, act, hidden)
 
 
-def shards(tokens, cotangent, routes, probs, slot_expert, gate_w, up_w, down_w):
+def shards_weights(tokens, cotangent, routes, probs, slot_expert, gate_w, up_w, down_w):
     n_exp = lax.axis_size("expert")
     local = gate_w.shape[0]
     tok_rows = tokens.shape[0]
@@ -108,6 +546,13 @@
         P("expert", "dp", None),
         P("expert", None, "dp"),
     )
+    n_dp, n_exp = mesh.shape["dp"], mesh.shape["expert"]
+
+    def shards(*args):
+        local, rows = args[5].shape[0], 2 * n_dp * CAP
+        by_rows = n_dp == 4 and local == 2 * n_dp and n_exp % 2 == 0 and n_exp > 2 and rows % 16 == 0
+        return (shards_rows if by_rows else shards_weights)(*args)
+
     return jax.shard_map(
         shards,
         mesh=mesh,

time: 1120 us -> 308 us (0.28)
  waiting for transfers between devices: 888 us -> 108 us
  matrix products: 121 us -> 0 us
  Pallas kernels: 0 us -> 120 us
  starting transfers between devices: 21.3 us -> 52.6 us
  other arithmetic: 31.3 us -> 3.67 us
  local copies, waits for them, and re-layouts: 28.4 us -> 4.16 us
  between operations: 14.9 us -> 1.06 us
    reduce_scatter x3 -> x0, waiting for transfers between devices: 485 us -> none  [the longest x1 226 us: shards(): lax.psum_scatter(part_up, 'dp', scatter_dimension=1, tiled=True)]
    all_to_all x4 -> x0, waiting for transfers between devices: 308 us -> none  [the longest x1 104 us: shards(): lax.all_to_all(dx_rows.reshape(n_exp, local * CAP, width), 'expert', spli...]
    dot_general x11 -> x0, matrix products: 121 us -> none  [the longest x1 15.8 us: shards(): jnp.einsum('sekd,sekf->edf', got_x, d_up, preferred_element_type=jnp.floa...]
    pallas_call x0 -> x19, Pallas kernels: none -> 120 us  [the longest x8 54.6 us: partials(): pl.pallas_call(kernel, grid_spec=pltpu.PrefetchScalarGridSpec(num_scalar_...]
    ppermute x0 -> x60, waiting for transfers between devices: none -> 108 us  [the longest x46 70 us: swap(): return lax.ppermute(a, 'dp', [(k, k ^ o) for k in range(n_dp)])]
    all_gather x3 -> x0, waiting for transfers between devices: 92.5 us -> none  [the longest x1 92.5 us: shards(): lax.all_gather(down_w, 'dp', axis=2, tiled=True)]
    ppermute x0 -> x60, starting transfers between devices: none -> 52.6 us  [the longest x46 50.3 us: swap(): return lax.ppermute(a, 'dp', [(k, k ^ o) for k in range(n_dp)])]
    all_to_all x4 -> x0, starting transfers between devices: 21.1 us -> none  [the longest x1 6.46 us: shards(): lax.all_to_all(send_x, 'expert', split_axis=0, concat_axis=0, tiled=True)]
  transfers between devices with their start and end apart: 10 -> 60, of which waited for: 8 -> 21; matrix products, arithmetic and copies ran while one was open for 13% -> 1% of each run, Pallas kernels for 0% -> 39%
where the time goes in v1:
time: 308 us; the launch traced here: 306 us
  Pallas kernels  120 us (39%)
  waiting for transfers between devices  108 us (35%)
  starting transfers between devices  52.6 us (17%)
  blocking collectives  16.7 us (5%)
  local copies, waits for them, and re-layouts  4.16 us (1%)
  other arithmetic  3.67 us (1%)
    ppermute x46, waiting for transfers between devices, swap(): return lax.ppermute(a, 'dp', [(k, k ^ o) for k in range(n_dp)])  70 us
    pallas_call x8, Pallas kernels, partials(): pl.pallas_call(kernel, grid_spec=pltpu.PrefetchScalarGridSpec(num_scalar_...  54.6 us
    ppermute x46, starting transfers between devices, swap(): return lax.ppermute(a, 'dp', [(k, k ^ o) for k in range(n_dp)])  50.3 us
    pallas_call x4, Pallas kernels, dx_chunk(): pl.pallas_call(dx_kernel, grid_spec=pltpu.PrefetchScalarGridSpec(num_scal...  41.7 us
    ppermute x6, waiting for transfers between devices, plane(): lax.ppermute(a, 'expert', [(k, (k + 2) % n_exp) for k in range(n_exp)])  36.1 us
    pallas_call x1, Pallas kernels, grads(): pl.pallas_call(grads_kernel, grid=(local,), in_specs=[spec(xs), spec(dys)...  16.8 us
    all_to_all x1, blocking collectives, shards_rows(): flat = lax.all_to_all(flat, ('dp', 'expert'), 0, 0, tiled=True)  16.7 us
  transfers between devices with their start and end apart: 60, of which 21 were waited for; matrix products, arithmetic and copies ran while one was open for 1% of the time, Pallas kernels for 39%

profile of v1, /device:TPU:0, one launch (start us, length us, event | category | flops | bytes accessed | tf_op | source)
XLA Modules:
  0.0 306.1 jit_solution(16483040540056501750)
XLA Ops:
  4.3 1.0 copy-done.1
  6.2 3.0 collective-permute-start
  9.2 1.5 collective-permute-start.1
  10.8 6.3 %collective-permute-done = bf16[128,1152]{1,0:T(8,128)(2,1)S(1)} collective-permute-done((bf16[128,1152]{1,0:T(8,128)(2,1)S(1)}, bf16[128,1152]{1,0:T(8,128)(2,1)S(1)}, u32[]{:S(2)}, u32[]{:S(2)}) %collective-permute-start) | collective-permute-done | bytes 294944 | tf_op jit(solution)/shard_map/ppermute | solution.py:390
  17.1 6.9 %collective-permute-done.1 = bf16[128,1152]{1,0:T(8,128)(2,1)S(1)} collective-permute-done((bf16[128,1152]{1,0:T(8,128)(2,1)S(1)}, bf16[128,1152]{1,0:T(8,128)(2,1)S(1)}, u32[]{:S(2)}, u32[]{:S(2)}) %collective-permute-start.1) | collective-permute-done | bytes 294944 | tf_op jit(solution)/shard_map/ppermute | solution.py:390
  24.1 1.6 collective-permute-start.15
  25.7 26.9 %collective-permute-done.15.refs_1_ = bf16[512,1152]{1,0:T(8,128)(2,1)S(1)} collective-permute-done((bf16[512,1152]{1,0:T(8,128)(2,1)S(1)}, bf16[512,1152]{1,0:T(8,128)(2,1)S(1)}, u32[]{:S(2)}, u32[]{:S(2)}) %collective-permute-start.15) | collective-permute-done | bytes 1179680 | tf_op jit(solution)/shard_map/ppermute | solution.py:396
  52.6 6.7 %partials_send.4 = (bf16[8,4,144,512]{3,2,1,0:T(8,128)(2,1)}, bf16[8,4,144,512]{3,2,1,0:T(8,128)(2,1)}, s32[4,1,1024]{2,1,0:T(1,128)S(1)}, bf16[1,144,1152]{2,1,...) custom-call(s32[15]{0:T(128)S(1)} %stack.63.info.refs_0_, ...), custom_call_target="tpu_custom_call" | custom-call | flops 1887436800 | bytes 8000000 | tf_op jit(solution)/shard_map/partials_send/pallas_call | solution.py:180
  59.8 1.5 collective-permute-start.5
  61.9 6.9 %partials_keep.4 = (bf16[8,4,144,512]{3,2,1,0:T(8,128)(2,1)}, bf16[8,4,144,512]{3,2,1,0:T(8,128)(2,1)}, s32[4,1,1024]{2,1,0:T(1,128)S(1)}, f32[4,144,1152]{2,1,0:T(8,128)S(1)}, f32[2,144,128]{2,1,0:T(8,128)S(1)}) custom-call(s32[15]{0:T(128)S(1)} %stack.63.info.refs_0_, ...), custom_call_target="tpu_custom_call", output_to_operand_aliasing={{0}: (6, {}), {1}: (7, {})} | custom-call | flops 1887436800 | bytes 8000000 | tf_op jit(solution)/shard_map/partials_keep/pallas_call | solution.py:180
  70.6 1.6 collective-permute-start.6
  72.2 1.4 collective-permute-start.9
  73.6 6.7 %partials_send.5 = (bf16[8,4,144,512]{3,2,1,0:T(8,128)(2,1)}, bf16[8,4,144,512]{3,2,1,0:T(8,128)(2,1)}, s32[4,1,1024]{2,1,0:T(1,128)S(1)}, bf16[1,144,1152]{2,1,...) custom-call(s32[15]{0:T(128)S(1)} %stack.63.info.refs_0_, ...), custom_call_target="tpu_custom_call", output_to_operand_aliasing={{0}: (6, {}), {1}: (7, {})} | custom-call | flops 1887436800 | bytes 8000000 | tf_op jit(solution)/shard_map/partials_send/pallas_call | solution.py:180
  81.7 9.3 %collective-permute-done.16.refs_1_ = bf16[512,1152]{1,0:T(8,128)(2,1)S(1)} collective-permute-done((bf16[512,1152]{1,0:T(8,128)(2,1)S(1)}, bf16[512,1152]{1,0:T(8,128)(2,1)S(1)}, u32[]{:S(2)}, u32[]{:S(2)}) %collective-permute-start.16) | collective-permute-done | bytes 1179680 | tf_op jit(solution)/shard_map/ppermute | solution.py:396
  91.0 1.2 inner.4
  93.2 1.1 collective-permute-start.11
  94.3 7.1 %partials_keep.5 = (bf16[8,4,144,512]{3,2,1,0:T(8,128)(2,1)}, bf16[8,4,144,512]{3,2,1,0:T(8,128)(2,1)}, s32[4,1,1024]{2,1,0:T(1,128)S(1)}, f32[4,144,1152]{2,1,0:T(8,128)S(1)}, f32[2,144,128]{2,1,0:T(8,128)S(1)}) custom-call(s32[15]{0:T(128)S(1)} %stack.63.info.refs_0_, ...), custom_call_target="tpu_custom_call", output_to_operand_aliasing={{0}: (6, {}), {1}: (7, {})} | custom-call | flops 1887436800 | bytes 8000000 | tf_op jit(solution)/shard_map/partials_keep/pallas_call | solution.py:180
  101.4 1.5 collective-permute-start.33
  103.0 6.9 %collective-permute-done.10.from_x = bf16[288,1152]{1,0:T(8,128)(2,1)S(1)} collective-permute-done((bf16[288,1152]{1,0:T(8,128)(2,1)S(1)}, bf16[288,1152]{1,0:T(8,128)(2,1)S(1)}, u32[]{:S(2)}, u32[]{:S(2)}) %collective-permute-start.10) | collective-permute-done | bytes 663584 | tf_op jit(solution)/shard_map/ppermute | solution.py:390
  109.9 1.5 collective-permute-start.36
  112.0 4.7 %collective-permute-done.33.raw_a = bf16[1,144,1152]{2,1,0:T(8,128)(2,1)S(1)} collective-permute-done((bf16[1,144,1152]{2,1,0:T(8,128)(2,1)S(1)}, bf16[1,144,1152]{2,1,0:T(8,128)(2,1)S(1)}, u32[]{:S(2)}, u32[]{:S(2)}) %collective-permute-start.33) | collective-permute-done | bytes 331808 | tf_op jit(solution)/shard_map/ppermute | solution.py:390
  117.2 3.5 %collective-permute-done.36.raw_b = bf16[1,144,1152]{2,1,0:T(8,128)(2,1)S(1)} collective-permute-done((bf16[1,144,1152]{2,1,0:T(8,128)(2,1)S(1)}, bf16[1,144,1152]{2,1,0:T(8,128)(2,1)S(1)}, u32[]{:S(2)}, u32[]{:S(2)}) %collective-permute-start.36) | collective-permute-done | bytes 331808 | tf_op jit(solution)/shard_map/ppermute | solution.py:390
  121.2 4.8 %collective-permute-done.35.sum_a = bf16[1,144,1152]{2,1,0:T(8,128)(2,1)S(1)} collective-permute-done((bf16[1,144,1152]{2,1,0:T(8,128)(2,1)S(1)}, bf16[1,144,1152]{2,1,0:T(8,128)(2,1)S(1)}, u32[]{:S(2)}, u32[]{:S(2)}) %collective-permute-start.35) | collective-permute-done | bytes 331808 | tf_op jit(solution)/shard_map/ppermute | solution.py:390
  126.1 1.5 collective-permute-start.13
  127.5 1.2 inner.5
  128.8 1.3 collective-permute-start.48
  130.7 6.7 %partials_send.6 = (bf16[8,4,144,512]{3,2,1,0:T(8,128)(2,1)}, bf16[8,4,144,512]{3,2,1,0:T(8,128)(2,1)}, s32[4,1,1024]{2,1,0:T(1,128)S(1)}, bf16[1,144,1152]{2,1,...) custom-call(s32[15]{0:T(128)S(1)} %stack.63.info.refs_0_, ...), custom_call_target="tpu_custom_call", output_to_operand_aliasing={{0}: (6, {}), {1}: (7, {})} | custom-call | flops 1887436800 | bytes 8000000 | tf_op jit(solution)/shard_map/partials_send/pallas_call | solution.py:180
  138.2 1.4 collective-permute-start.28
  139.6 10.3 %dx.4 = (bf16[8,4,144,1152]{3,2,1,0:T(8,128)(2,1)}, f32[512,512]{1,0:T(8,128)S(1)}, bf16[512,512]{1,0:T(8,128)(2,1)S(1)}) custom-call(s32[15]{0:T(128)S(1)} %stack.63.info.refs_0_, bf16[288,1152]{1,0:T(8,128)(2,1)S(1)} %get-tuple-element.93.own, bf16[288,1152]{1,0:T(8,128)(2,1)S(1)} %collective-permute-done.10.from_x, ...), custom_call_target="tpu_custom_call" | custom-call | flops 2113929216 | bytes 12000000 | tf_op jit(solution)/shard_map/dx/pallas_call | solution.py:304
  150.0 6.9 %partials_keep.6 = (bf16[8,4,144,512]{3,2,1,0:T(8,128)(2,1)}, bf16[8,4,144,512]{3,2,1,0:T(8,128)(2,1)}, s32[4,1,1024]{2,1,0:T(1,128)S(1)}, f32[4,144,1152]{2,1,0:T(8,128)S(1)}, f32[2,144,128]{2,1,0:T(8,128)S(1)}) custom-call(s32[15]{0:T(128)S(1)} %stack.63.info.refs_0_, ...), custom_call_target="tpu_custom_call", output_to_operand_aliasing={{0}: (6, {}), {1}: (7, {})} | custom-call | flops 1887436800 | bytes 8000000 | tf_op jit(solution)/shard_map/partials_keep/pallas_call | solution.py:180
  157.6 1.3 collective-permute-start.30
  159.0 1.5 collective-permute-start.49
  162.1 5.5 %collective-permute-done.27.raw_a = bf16[1,144,1152]{2,1,0:T(8,128)(2,1)S(1)} collective-permute-done((bf16[1,144,1152]{2,1,0:T(8,128)(2,1)S(1)}, bf16[1,144,1152]{2,1,0:T(8,128)(2,1)S(1)}, u32[]{:S(2)}, u32[]{:S(2)}) %collective-permute-start.27) | collective-permute-done | bytes 331808 | tf_op jit(solution)/shard_map/ppermute | solution.py:390
  167.6 1.3 collective-permute-start.29
  169.5 6.7 %partials_send.7 = (bf16[8,4,144,512]{3,2,1,0:T(8,128)(2,1)}, bf16[8,4,144,512]{3,2,1,0:T(8,128)(2,1)}, s32[4,1,1024]{2,1,0:T(1,128)S(1)}, bf16[1,144,1152]{2,1,...) custom-call(s32[15]{0:T(128)S(1)} %stack.63.info.refs_0_, ...), custom_call_target="tpu_custom_call", output_to_operand_aliasing={{0}: (6, {}), {1}: (7, {})} | custom-call | flops 1887436800 | bytes 8000000 | tf_op jit(solution)/shard_map/partials_send/pallas_call | solution.py:180
  177.0 1.4 collective-permute-start.22
  178.4 10.4 %dx.5 = (bf16[8,4,144,1152]{3,2,1,0:T(8,128)(2,1)}, f32[512,512]{1,0:T(8,128)S(1)}, bf16[512,512]{1,0:T(8,128)(2,1)S(1)}) custom-call(s32[15]{0:T(128)S(1)} %stack.63.info.refs_0_, bf16[288,1152]{1,0:T(8,128)(2,1)S(1)} %get-tuple-element.137.own, bf16[288,1152]{1,0:T(8,128)(2,1)S(1)} %collective-permute-done.47.from_x, ...), custom_call_target="tpu_custom_call", output_to_operand_aliasing={{0}: (10, {})} | custom-call | flops 2113929216 | bytes 12000000 | tf_op jit(solution)/shard_map/dx/pallas_call | solution.py:304
  188.8 1.2 inner.6
  190.8 1.2 collective-permute-start.44
  192.0 6.9 %partials_keep.7 = (bf16[8,4,144,512]{3,2,1,0:T(8,128)(2,1)}, bf16[8,4,144,512]{3,2,1,0:T(8,128)(2,1)}, s32[4,1,1024]{2,1,0:T(1,128)S(1)}, f32[4,144,1152]{2,1,0:T(8,128)S(1)}, f32[2,144,128]{2,1,0:T(8,128)S(1)}) custom-call(s32[15]{0:T(128)S(1)} %stack.63.info.refs_0_, ...), custom_call_target="tpu_custom_call", output_to_operand_aliasing={{0}: (6, {}), {1}: (7, {})} | custom-call | flops 1887436800 | bytes 8000000 | tf_op jit(solution)/shard_map/partials_keep/pallas_call | solution.py:180
  198.9 1.5 collective-permute-start.21
  201.3 6.5 %collective-permute-done.43.from_x = bf16[288,1152]{1,0:T(8,128)(2,1)S(1)} collective-permute-done((bf16[288,1152]{1,0:T(8,128)(2,1)S(1)}, bf16[288,1152]{1,0:T(8,128)(2,1)S(1)}, u32[]{:S(2)}, u32[]{:S(2)}) %collective-permute-start.43) | collective-permute-done | bytes 663584 | tf_op jit(solution)/shard_map/ppermute | solution.py:390
  207.8 1.3 collective-permute-start.23
  209.9 1.3 collective-permute-start.45
  211.3 3.6 %collective-permute-done.21.raw_a = bf16[1,144,1152]{2,1,0:T(8,128)(2,1)S(1)} collective-permute-done((bf16[1,144,1152]{2,1,0:T(8,128)(2,1)S(1)}, bf16[1,144,1152]{2,1,0:T(8,128)(2,1)S(1)}, u32[]{:S(2)}, u32[]{:S(2)}) %collective-permute-start.21) | collective-permute-done | bytes 331808 | tf_op jit(solution)/shard_map/ppermute | solution.py:390
  214.9 1.3 collective-permute-start.46
  216.4 6.3 %collective-permute-done.23.sum_a = bf16[1,144,1152]{2,1,0:T(8,128)(2,1)S(1)} collective-permute-done((bf16[1,144,1152]{2,1,0:T(8,128)(2,1)S(1)}, bf16[1,144,1152]{2,1,0:T(8,128)(2,1)S(1)}, u32[]{:S(2)}, u32[]{:S(2)}) %collective-permute-start.23) | collective-permute-done | bytes 331808 | tf_op jit(solution)/shard_map/ppermute | solution.py:390
  222.7 1.2 inner.7
  224.0 1.4 collective-permute-start.39
  225.4 1.3 collective-permute-start.40
  226.7 2.5 collective-permute-done.45.far_a
  229.8 10.4 %dx.6 = (bf16[8,4,144,1152]{3,2,1,0:T(8,128)(2,1)}, f32[512,512]{1,0:T(8,128)S(1)}, bf16[512,512]{1,0:T(8,128)(2,1)S(1)}) custom-call(s32[15]{0:T(128)S(1)} %stack.63.info.refs_0_, bf16[288,1152]{1,0:T(8,128)(2,1)S(1)} %get-tuple-element.135.own, bf16[288,1152]{1,0:T(8,128)(2,1)S(1)} %collective-permute-done.43.from_x, ...), custom_call_target="tpu_custom_call", output_to_operand_aliasing={{0}: (10, {})} | custom-call | flops 2113929216 | bytes 12000000 | tf_op jit(solution)/shard_map/dx/pallas_call | solution.py:304
  240.2 3.1 %collective-permute-done.40.from_y = bf16[288,1152]{1,0:T(8,128)(2,1)S(1)} collective-permute-done((bf16[288,1152]{1,0:T(8,128)(2,1)S(1)}, bf16[288,1152]{1,0:T(8,128)(2,1)S(1)}, u32[]{:S(2)}, u32[]{:S(2)}) %collective-permute-start.40) | collective-permute-done | bytes 663584 | tf_op jit(solution)/shard_map/ppermute | solution.py:390
  243.4 1.4 collective-permute-start.41
  244.8 1.4 collective-permute-start.42
  246.5 6.1 %collective-permute-done.41.far_a = bf16[144,1152]{1,0:T(8,128)(2,1)S(1)} collective-permute-done((bf16[144,1152]{1,0:T(8,128)(2,1)S(1)}, bf16[144,1152]{1,0:T(8,128)(2,1)S(1)}, u32[]{:S(2)}, u32[]{:S(2)}) %collective-permute-start.41) | collective-permute-done | bytes 331808 | tf_op jit(solution)/shard_map/ppermute | solution.py:390
  252.5 1.2 collective-permute-done.42.far_b
  253.7 10.7 %dx.7 = (bf16[8,4,144,1152]{3,2,1,0:T(8,128)(2,1)}, f32[512,512]{1,0:T(8,128)S(1)}, bf16[512,512]{1,0:T(8,128)(2,1)S(1)}) custom-call(s32[15]{0:T(128)S(1)} %stack.63.info.refs_0_, bf16[288,1152]{1,0:T(8,128)(2,1)S(1)} %get-tuple-element.133.own, bf16[288,1152]{1,0:T(8,128)(2,1)S(1)} %collective-permute-done.39.from_x, ...), custom_call_target="tpu_custom_call", output_to_operand_aliasing={{0}: (10, {})} | custom-call | flops 2113929216 | bytes 12000000 | tf_op jit(solution)/shard_map/dx/pallas_call | solution.py:304
  264.9 1.4 collective-permute-done.51
  266.6 16.7 %all_to_all.5 = bf16[32,2,128]{2,1,0:T(2,128)(2,1)S(1)} all-to-all(bf16[32,2,128]{2,1,0:T(2,128)(2,1)S(1)} %bitcast.28), channel_id=1, replica_groups=mesh['dp'=4,'expert'=8] {'dp','expert'}, dimensions={0} | all-to-all | bytes 32768 | tf_op jit(solution)/shard_map/all_to_all | solution.py:440
  284.3 1.6 collective-permute-start.57
  286.6 1.3 collective-permute-start.59
  287.9 16.8 %grads.1 = (f32[8,512,384]{2,1,0:T(8,128)}, f32[8,512,384]{2,1,0:T(8,128)}, f32[8,384,512]{2,1,0:T(8,128)}) custom-call(bf16[8,4,144,512]{3,2,1,0:T(8,128)(2,1)S(1)} %bitcast.27, bf16[8,4,144,512]{3,2,1,0:T(8,128)(2,1)} %get-tuple-element.150.dys, bf16[8,4,144,1152]{3,2,1,0:T(8,128)(2,1)} %get-tuple-element.151.acts), custom_call_target="tpu_custom_call" | custom-call | flops 5435817984 | bytes 30000000 | tf_op jit(solution)/shard_map/grads/pallas_call | solution.py:344
  304.7 1.4 join.1
  (118 shorter events, 23.2 us)
Async XLA Ops:
  6.2 10.8 %collective-permute-start = (bf16[128,1152]{1,0:T(8,128)(2,1)S(1)}, bf16[128,1152]{1,0:T(8,128)(2,1)S(1)}, u32[]{:S(2)}, u32[]{:S(2)}) collective-permute-start(bf16[128,1152]{1,0:T(8,128)(2,1)S(1)} %get-tuple-element.81), channel_id=1, source_target_pairs={{0,8},{8,0},{16,24},{24,16},{1,9},{9,1},{17,25},{25,17},{2,10},{10... | collective-permute-start | bytes 884744 | tf_op jit(solution)/shard_map/ppermute | solution.py:390
  9.2 14.8 %collective-permute-start.1 = (bf16[128,1152]{1,0:T(8,128)(2,1)S(1)}, bf16[128,1152]{1,0:T(8,128)(2,1)S(1)}, u32[]{:S(2)}, u32[]{:S(2)}) collective-permute-start(bf16[128,1152]{1,0:T(8,128)(2,1)S(1)} %get-tuple-element.82), channel_id=1, source_target_pairs={{0,16},{8,24},{16,0},{24,8},{1,17},{9,25},{17,1},{25,9},{2,18},{10... | collective-permute-start | bytes 884744 | tf_op jit(solution)/shard_map/ppermute | solution.py:390
  10.8 13.3 %collective-permute-start.2 = (bf16[128,1152]{1,0:T(8,128)(2,1)S(1)}, bf16[128,1152]{1,0:T(8,128)(2,1)S(1)}, u32[]{:S(2)}, u32[]{:S(2)}) collective-permute-start(bf16[128,1152]{1,0:T(8,128)(2,1)S(1)} %get-tuple-element.83), channel_id=1, source_target_pairs={{0,24},{8,16},{16,8},{24,0},{1,25},{9,17},{17,9},{25,1},{2,26},{10... | collective-permute-start | bytes 884744 | tf_op jit(solution)/shard_map/ppermute | solution.py:390
  24.1 28.5 %collective-permute-start.15 = (bf16[512,1152]{1,0:T(8,128)(2,1)S(1)}, bf16[512,1152]{1,0:T(8,128)(2,1)S(1)}, u32[]{:S(2)}, u32[]{:S(2)}) collective-permute-start(bf16[512,1152]{1,0:T(8,128)(2,1)S(1)} %constant_dynamic-update-slice_fusion.refs_1_), channel_id=1, source_target_pairs={{0,2},{1,3},{2,4},{3,5},{4,6},{5,7},{6,0},{7,1},{8,10},{9,11},{10,... | collective-permute-start | bytes 3538952 | tf_op jit(solution)/shard_map/ppermute | solution.py:396
  25.7 26.9 %collective-permute-start.3 = (bf16[512,1152]{1,0:T(8,128)(2,1)S(1)}, bf16[512,1152]{1,0:T(8,128)(2,1)S(1)}, u32[]{:S(2)}, u32[]{:S(2)}) collective-permute-start(bf16[512,1152]{1,0:T(8,128)(2,1)S(1)} %constant_dynamic-update-slice_fusion.refs_1_), channel_id=1, source_target_pairs={{0,1},{1,0},{2,3},{3,2},{4,5},{5,4},{6,7},{7,6},{8,9},{9,8},{10,11... | collective-permute-start | bytes 3538952 | tf_op jit(solution)/shard_map/ppermute | solution.py:393
  52.6 19.6 %collective-permute-start.20 = (bf16[512,1152]{1,0:T(8,128)(2,1)S(1)}, bf16[512,1152]{1,0:T(8,128)(2,1)S(1)}, u32[]{:S(2)}, u32[]{:S(2)}) collective-permute-start(bf16[512,1152]{1,0:T(8,128)(2,1)S(1)} %collective-permute-done.15.refs_1_), channel_id=1, source_target_pairs={{0,1},{1,0},{2,3},{3,2},{4,5},{5,4},{6,7},{7,6},{8,9},{9,8},{10,11... | collective-permute-start | bytes 3538952 | tf_op jit(solution)/shard_map/ppermute | solution.py:393
  59.3 10.2 %collective-permute-start.8 = (bf16[1,144,1152]{2,1,0:T(8,128)(2,1)S(1)}, bf16[1,144,1152]{2,1,0:T(8,128)(2,1)S(1)}, u32[]{:S(2)}, u32[]{:S(2)}) collective-permute-start(bf16[1,144,1152]{2,1,0:T(8,128)(2,1)S(1)} %get-tuple-element.90), channel_id=1, source_target_pairs={{0,16},{8,24},{16,0},{24,8},{1,17},{9,25},{17,1},{25,9},{2,18},{10... | collective-permute-start | bytes 995336 | tf_op jit(solution)/shard_map/ppermute | solution.py:390
  59.8 10.6 %collective-permute-start.5 = (bf16[1,144,1152]{2,1,0:T(8,128)(2,1)S(1)}, bf16[1,144,1152]{2,1,0:T(8,128)(2,1)S(1)}, u32[]{:S(2)}, u32[]{:S(2)}) collective-permute-start(bf16[1,144,1152]{2,1,0:T(8,128)(2,1)S(1)} %get-tuple-element.88), channel_id=1, source_target_pairs={{0,8},{8,0},{16,24},{24,16},{1,9},{9,1},{17,25},{25,17},{2,10},{10... | collective-permute-start | bytes 995336 | tf_op jit(solution)/shard_map/ppermute | solution.py:390
  61.3 29.6 %collective-permute-start.16 = (bf16[512,1152]{1,0:T(8,128)(2,1)S(1)}, bf16[512,1152]{1,0:T(8,128)(2,1)S(1)}, u32[]{:S(2)}, u32[]{:S(2)}) collective-permute-start(bf16[512,1152]{1,0:T(8,128)(2,1)S(1)} %collective-permute-done.15.refs_1_), channel_id=1, source_target_pairs={{0,2},{1,3},{2,4},{3,5},{4,6},{5,7},{6,0},{7,1},{8,10},{9,11},{10,... | collective-permute-start | bytes 3538952 | tf_op jit(solution)/shard_map/ppermute | solution.py:396
  61.3 19.0 %collective-permute-start.4 = (bf16[1,144,1152]{2,1,0:T(8,128)(2,1)S(1)}, bf16[1,144,1152]{2,1,0:T(8,128)(2,1)S(1)}, u32[]{:S(2)}, u32[]{:S(2)}) collective-permute-start(bf16[1,144,1152]{2,1,0:T(8,128)(2,1)S(1)} %get-tuple-element.87), channel_id=1, source_target_pairs={{0,8},{8,0},{16,24},{24,16},{1,9},{9,1},{17,25},{25,17},{2,10},{10... | collective-permute-start | bytes 995336 | tf_op jit(solution)/shard_map/ppermute | solution.py:390
  69.5 11.4 %collective-permute-start.7 = (bf16[1,144,1152]{2,1,0:T(8,128)(2,1)S(1)}, bf16[1,144,1152]{2,1,0:T(8,128)(2,1)S(1)}, u32[]{:S(2)}, u32[]{:S(2)}) collective-permute-start(bf16[1,144,1152]{2,1,0:T(8,128)(2,1)S(1)} %get-tuple-element.89), channel_id=1, source_target_pairs={{0,16},{8,24},{16,0},{24,8},{1,17},{9,25},{17,1},{25,9},{2,18},{10... | collective-permute-start | bytes 995336 | tf_op jit(solution)/shard_map/ppermute | solution.py:390
  70.6 20.3 %collective-permute-start.6 = (bf16[1,144,1152]{2,1,0:T(8,128)(2,1)S(1)}, bf16[1,144,1152]{2,1,0:T(8,128)(2,1)S(1)}, u32[]{:S(2)}, u32[]{:S(2)}) collective-permute-start(bf16[1,144,1152]{2,1,0:T(8,128)(2,1)S(1)} %get-tuple-element.160), channel_id=1, source_target_pairs={{0,16},{8,24},{16,0},{24,8},{1,17},{9,25},{17,1},{25,9},{2,18},{10... | collective-permute-start | bytes 995336 | tf_op jit(solution)/shard_map/ppermute | solution.py:390
  72.2 18.7 %collective-permute-start.9 = (bf16[1,144,1152]{2,1,0:T(8,128)(2,1)S(1)}, bf16[1,144,1152]{2,1,0:T(8,128)(2,1)S(1)}, u32[]{:S(2)}, u32[]{:S(2)}) collective-permute-start(bf16[1,144,1152]{2,1,0:T(8,128)(2,1)S(1)} %get-tuple-element.159), channel_id=1, source_target_pairs={{0,8},{8,0},{16,24},{24,16},{1,9},{9,1},{17,25},{25,17},{2,10},{10... | collective-permute-start | bytes 995336 | tf_op jit(solution)/shard_map/ppermute | solution.py:390
  80.3 12.8 %collective-permute-start.37 = (bf16[1,144,1152]{2,1,0:T(8,128)(2,1)S(1)}, bf16[1,144,1152]{2,1,0:T(8,128)(2,1)S(1)}, u32[]{:S(2)}, u32[]{:S(2)}) collective-permute-start(bf16[1,144,1152]{2,1,0:T(8,128)(2,1)S(1)} %get-tuple-element.127), channel_id=1, source_target_pairs={{0,16},{8,24},{16,0},{24,8},{1,17},{9,25},{17,1},{25,9},{2,18},{10... | collective-permute-start | bytes 995336 | tf_op jit(solution)/shard_map/ppermute | solution.py:390
  80.9 20.5 %collective-permute-start.34 = (bf16[1,144,1152]{2,1,0:T(8,128)(2,1)S(1)}, bf16[1,144,1152]{2,1,0:T(8,128)(2,1)S(1)}, u32[]{:S(2)}, u32[]{:S(2)}) collective-permute-start(bf16[1,144,1152]{2,1,0:T(8,128)(2,1)S(1)} %get-tuple-element.125), channel_id=1, source_target_pairs={{0,8},{8,0},{16,24},{24,16},{1,9},{9,1},{17,25},{25,17},{2,10},{10... | collective-permute-start | bytes 995336 | tf_op jit(solution)/shard_map/ppermute | solution.py:390
  90.9 39.2 %collective-permute-start.19 = (bf16[512,1152]{1,0:T(8,128)(2,1)S(1)}, bf16[512,1152]{1,0:T(8,128)(2,1)S(1)}, u32[]{:S(2)}, u32[]{:S(2)}) collective-permute-start(bf16[512,1152]{1,0:T(8,128)(2,1)S(1)} %collective-permute-done.16.refs_1_), channel_id=1, source_target_pairs={{0,1},{1,0},{2,3},{3,2},{4,5},{5,4},{6,7},{7,6},{8,9},{9,8},{10,11... | collective-permute-start | bytes 3538952 | tf_op jit(solution)/shard_map/ppermute | solution.py:393
  90.9 39.8 %collective-permute-start.17 = (bf16[512,1152]{1,0:T(8,128)(2,1)S(1)}, bf16[512,1152]{1,0:T(8,128)(2,1)S(1)}, u32[]{:S(2)}, u32[]{:S(2)}) collective-permute-start(bf16[512,1152]{1,0:T(8,128)(2,1)S(1)} %collective-permute-done.16.refs_1_), channel_id=1, source_target_pairs={{0,2},{1,3},{2,4},{3,5},{4,6},{5,7},{6,0},{7,1},{8,10},{9,11},{10,... | collective-permute-start | bytes 3538952 | tf_op jit(solution)/shard_map/ppermute | solution.py:396
  92.2 17.8 %collective-permute-start.10 = (bf16[288,1152]{1,0:T(8,128)(2,1)S(1)}, bf16[288,1152]{1,0:T(8,128)(2,1)S(1)}, u32[]{:S(2)}, u32[]{:S(2)}) collective-permute-start(bf16[288,1152]{1,0:T(8,128)(2,1)S(1)} %get-tuple-element.93.own), channel_id=1, source_target_pairs={{0,8},{8,0},{16,24},{24,16},{1,9},{9,1},{17,25},{25,17},{2,10},{10... | collective-permute-start | bytes 1990664 | tf_op jit(solution)/shard_map/ppermute | solution.py:390
  93.2 18.2 %collective-permute-start.11 = (bf16[288,1152]{1,0:T(8,128)(2,1)S(1)}, bf16[288,1152]{1,0:T(8,128)(2,1)S(1)}, u32[]{:S(2)}, u32[]{:S(2)}) collective-permute-start(bf16[288,1152]{1,0:T(8,128)(2,1)S(1)} %get-tuple-element.93.own), channel_id=1, source_target_pairs={{0,16},{8,24},{16,0},{24,8},{1,17},{9,25},{17,1},{25,9},{2,18},{10... | collective-permute-start | bytes 1990664 | tf_op jit(solution)/shard_map/ppermute | solution.py:390
  101.4 15.3 %collective-permute-start.33 = (bf16[1,144,1152]{2,1,0:T(8,128)(2,1)S(1)}, bf16[1,144,1152]{2,1,0:T(8,128)(2,1)S(1)}, u32[]{:S(2)}, u32[]{:S(2)}) collective-permute-start(bf16[1,144,1152]{2,1,0:T(8,128)(2,1)S(1)} %get-tuple-element.124), channel_id=1, source_target_pairs={{0,8},{8,0},{16,24},{24,16},{1,9},{9,1},{17,25},{25,17},{2,10},{10... | collective-permute-start | bytes 995336 | tf_op jit(solution)/shard_map/ppermute | solution.py:390
  109.9 10.7 %collective-permute-start.36 = (bf16[1,144,1152]{2,1,0:T(8,128)(2,1)S(1)}, bf16[1,144,1152]{2,1,0:T(8,128)(2,1)S(1)}, u32[]{:S(2)}, u32[]{:S(2)}) collective-permute-start(bf16[1,144,1152]{2,1,0:T(8,128)(2,1)S(1)} %get-tuple-element.126), channel_id=1, source_target_pairs={{0,16},{8,24},{16,0},{24,8},{1,17},{9,25},{17,1},{25,9},{2,18},{10... | collective-permute-start | bytes 995336 | tf_op jit(solution)/shard_map/ppermute | solution.py:390
  111.4 14.7 %collective-permute-start.35 = (bf16[1,144,1152]{2,1,0:T(8,128)(2,1)S(1)}, bf16[1,144,1152]{2,1,0:T(8,128)(2,1)S(1)}, u32[]{:S(2)}, u32[]{:S(2)}) collective-permute-start(bf16[1,144,1152]{2,1,0:T(8,128)(2,1)S(1)} %get-tuple-element.162), channel_id=1, source_target_pairs={{0,16},{8,24},{16,0},{24,8},{1,17},{9,25},{17,1},{25,9},{2,18},{10... | collective-permute-start | bytes 995336 | tf_op jit(solution)/shard_map/ppermute | solution.py:390
  116.7 10.9 %collective-permute-start.38 = (bf16[1,144,1152]{2,1,0:T(8,128)(2,1)S(1)}, bf16[1,144,1152]{2,1,0:T(8,128)(2,1)S(1)}, u32[]{:S(2)}, u32[]{:S(2)}) collective-permute-start(bf16[1,144,1152]{2,1,0:T(8,128)(2,1)S(1)} %get-tuple-element.161), channel_id=1, source_target_pairs={{0,8},{8,0},{16,24},{24,16},{1,9},{9,1},{17,25},{25,17},{2,10},{10... | collective-permute-start | bytes 995336 | tf_op jit(solution)/shard_map/ppermute | solution.py:390
  120.7 16.8 %collective-permute-start.12 = (bf16[144,1152]{1,0:T(8,128)(2,1)S(1)}, bf16[144,1152]{1,0:T(8,128)(2,1)S(1)}, u32[]{:S(2)}, u32[]{:S(2)}) collective-permute-start(bf16[144,1152]{1,0:T(8,128)(2,1)S(1)} %slice.80), channel_id=1, source_target_pairs={{0,8},{8,0},{16,24},{24,16},{1,9},{9,1},{17,25},{25,17},{2,10},{10... | collective-permute-start | bytes 995336 | tf_op jit(solution)/shard_map/ppermute | solution.py:390
  126.1 12.1 %collective-permute-start.13 = (bf16[144,1152]{1,0:T(8,128)(2,1)S(1)}, bf16[144,1152]{1,0:T(8,128)(2,1)S(1)}, u32[]{:S(2)}, u32[]{:S(2)}) collective-permute-start(bf16[144,1152]{1,0:T(8,128)(2,1)S(1)} %slice.81), channel_id=1, source_target_pairs={{0,16},{8,24},{16,0},{24,8},{1,17},{9,25},{17,1},{25,9},{2,18},{10... | collective-permute-start | bytes 995336 | tf_op jit(solution)/shard_map/ppermute | solution.py:390
  128.8 28.1 %collective-permute-start.48 = (bf16[288,1152]{1,0:T(8,128)(2,1)S(1)}, bf16[288,1152]{1,0:T(8,128)(2,1)S(1)}, u32[]{:S(2)}, u32[]{:S(2)}) collective-permute-start(bf16[288,1152]{1,0:T(8,128)(2,1)S(1)} %get-tuple-element.137.own), channel_id=1, source_target_pairs={{0,16},{8,24},{16,0},{24,8},{1,17},{9,25},{17,1},{25,9},{2,18},{10... | collective-permute-start | bytes 1990664 | tf_op jit(solution)/shard_map/ppermute | solution.py:390
  130.1 27.5 %collective-permute-start.47 = (bf16[288,1152]{1,0:T(8,128)(2,1)S(1)}, bf16[288,1152]{1,0:T(8,128)(2,1)S(1)}, u32[]{:S(2)}, u32[]{:S(2)}) collective-permute-start(bf16[288,1152]{1,0:T(8,128)(2,1)S(1)} %get-tuple-element.137.own), channel_id=1, source_target_pairs={{0,8},{8,0},{16,24},{24,16},{1,9},{9,1},{17,25},{25,17},{2,10},{10... | collective-permute-start | bytes 1990664 | tf_op jit(solution)/shard_map/ppermute | solution.py:390
  130.7 38.2 %collective-permute-start.18 = (bf16[512,1152]{1,0:T(8,128)(2,1)S(1)}, bf16[512,1152]{1,0:T(8,128)(2,1)S(1)}, u32[]{:S(2)}, u32[]{:S(2)}) collective-permute-start(bf16[512,1152]{1,0:T(8,128)(2,1)S(1)} %collective-permute-done.17.refs_1_), channel_id=1, source_target_pairs={{0,1},{1,0},{2,3},{3,2},{4,5},{5,4},{6,7},{7,6},{8,9},{9,8},{10,11... | collective-permute-start | bytes 3538952 | tf_op jit(solution)/shard_map/ppermute | solution.py:393
  137.4 21.5 %collective-permute-start.31 = (bf16[1,144,1152]{2,1,0:T(8,128)(2,1)S(1)}, bf16[1,144,1152]{2,1,0:T(8,128)(2,1)S(1)}, u32[]{:S(2)}, u32[]{:S(2)}) collective-permute-start(bf16[1,144,1152]{2,1,0:T(8,128)(2,1)S(1)} %get-tuple-element.120), channel_id=1, source_target_pairs={{0,16},{8,24},{16,0},{24,8},{1,17},{9,25},{17,1},{25,9},{2,18},{10... | collective-permute-start | bytes 995336 | tf_op jit(solution)/shard_map/ppermute | solution.py:390
  138.2 22.2 %collective-permute-start.28 = (bf16[1,144,1152]{2,1,0:T(8,128)(2,1)S(1)}, bf16[1,144,1152]{2,1,0:T(8,128)(2,1)S(1)}, u32[]{:S(2)}, u32[]{:S(2)}) collective-permute-start(bf16[1,144,1152]{2,1,0:T(8,128)(2,1)S(1)} %get-tuple-element.118), channel_id=1, source_target_pairs={{0,8},{8,0},{16,24},{24,16},{1,9},{9,1},{17,25},{25,17},{2,10},{10... | collective-permute-start | bytes 995336 | tf_op jit(solution)/shard_map/ppermute | solution.py:390
  156.9 10.7 %collective-permute-start.27 = (bf16[1,144,1152]{2,1,0:T(8,128)(2,1)S(1)}, bf16[1,144,1152]{2,1,0:T(8,128)(2,1)S(1)}, u32[]{:S(2)}, u32[]{:S(2)}) collective-permute-start(bf16[1,144,1152]{2,1,0:T(8,128)(2,1)S(1)} %get-tuple-element.117), channel_id=1, source_target_pairs={{0,8},{8,0},{16,24},{24,16},{1,9},{9,1},{17,25},{25,17},{2,10},{10... | collective-permute-start | bytes 995336 | tf_op jit(solution)/shard_map/ppermute | solution.py:390
  157.6 31.1 %collective-permute-start.30 = (bf16[1,144,1152]{2,1,0:T(8,128)(2,1)S(1)}, bf16[1,144,1152]{2,1,0:T(8,128)(2,1)S(1)}, u32[]{:S(2)}, u32[]{:S(2)}) collective-permute-start(bf16[1,144,1152]{2,1,0:T(8,128)(2,1)S(1)} %get-tuple-element.119), channel_id=1, source_target_pairs={{0,16},{8,24},{16,0},{24,8},{1,17},{9,25},{17,1},{25,9},{2,18},{10... | collective-permute-start | bytes 995336 | tf_op jit(solution)/shard_map/ppermute | solution.py:390
  159.0 17.2 %collective-permute-start.49 = (bf16[144,1152]{1,0:T(8,128)(2,1)S(1)}, bf16[144,1152]{1,0:T(8,128)(2,1)S(1)}, u32[]{:S(2)}, u32[]{:S(2)}) collective-permute-start(bf16[144,1152]{1,0:T(8,128)(2,1)S(1)} %slice.86), channel_id=1, source_target_pairs={{0,8},{8,0},{16,24},{24,16},{1,9},{9,1},{17,25},{25,17},{2,10},{10... | collective-permute-start | bytes 995336 | tf_op jit(solution)/shard_map/ppermute | solution.py:390
  160.4 16.6 %collective-permute-start.50 = (bf16[144,1152]{1,0:T(8,128)(2,1)S(1)}, bf16[144,1152]{1,0:T(8,128)(2,1)S(1)}, u32[]{:S(2)}, u32[]{:S(2)}) collective-permute-start(bf16[144,1152]{1,0:T(8,128)(2,1)S(1)} %slice.87), channel_id=1, source_target_pairs={{0,16},{8,24},{16,0},{24,8},{1,17},{9,25},{17,1},{25,9},{2,18},{10... | collective-permute-start | bytes 995336 | tf_op jit(solution)/shard_map/ppermute | solution.py:390
  167.6 21.2 %collective-permute-start.29 = (bf16[1,144,1152]{2,1,0:T(8,128)(2,1)}, bf16[1,144,1152]{2,1,0:T(8,128)(2,1)S(1)}, u32[]{:S(2)}, u32[]{:S(2)}) collective-permute-start(bf16[1,144,1152]{2,1,0:T(8,128)(2,1)} %get-tuple-element.158), channel_id=1, source_target_pairs={{0,16},{8,24},{16,0},{24,8},{1,17},{9,25},{17,1},{25,9},{2,18},{10... | collective-permute-start | bytes 995336 | tf_op jit(solution)/shard_map/ppermute | solution.py:390
  168.9 19.9 %collective-permute-start.32 = (bf16[1,144,1152]{2,1,0:T(8,128)(2,1)S(1)}, bf16[1,144,1152]{2,1,0:T(8,128)(2,1)S(1)}, u32[]{:S(2)}, u32[]{:S(2)}) collective-permute-start(bf16[1,144,1152]{2,1,0:T(8,128)(2,1)S(1)} %get-tuple-element.157), channel_id=1, source_target_pairs={{0,8},{8,0},{16,24},{24,16},{1,9},{9,1},{17,25},{25,17},{2,10},{10... | collective-permute-start | bytes 995336 | tf_op jit(solution)/shard_map/ppermute | solution.py:390
  176.2 22.7 %collective-permute-start.25 = (bf16[1,144,1152]{2,1,0:T(8,128)(2,1)S(1)}, bf16[1,144,1152]{2,1,0:T(8,128)(2,1)S(1)}, u32[]{:S(2)}, u32[]{:S(2)}) collective-permute-start(bf16[1,144,1152]{2,1,0:T(8,128)(2,1)S(1)} %get-tuple-element.113), channel_id=1, source_target_pairs={{0,16},{8,24},{16,0},{24,8},{1,17},{9,25},{17,1},{25,9},{2,18},{10... | collective-permute-start | bytes 995336 | tf_op jit(solution)/shard_map/ppermute | solution.py:390
  177.0 23.3 %collective-permute-start.22 = (bf16[1,144,1152]{2,1,0:T(8,128)(2,1)S(1)}, bf16[1,144,1152]{2,1,0:T(8,128)(2,1)S(1)}, u32[]{:S(2)}, u32[]{:S(2)}) collective-permute-start(bf16[1,144,1152]{2,1,0:T(8,128)(2,1)S(1)} %get-tuple-element.111), channel_id=1, source_target_pairs={{0,8},{8,0},{16,24},{24,16},{1,9},{9,1},{17,25},{25,17},{2,10},{10... | collective-permute-start | bytes 995336 | tf_op jit(solution)/shard_map/ppermute | solution.py:390
  188.8 21.2 %collective-permute-start.53 = (bf16[512,512]{1,0:T(8,128)(2,1)S(1)}, bf16[512,512]{1,0:T(8,128)(2,1)S(1)}, u32[]{:S(2)}, u32[]{:S(2)}) collective-permute-start(bf16[512,512]{1,0:T(8,128)(2,1)S(1)} %get-tuple-element.147), channel_id=1, source_target_pairs={{0,1},{1,0},{2,3},{3,2},{4,5},{5,4},{6,7},{7,6},{8,9},{9,8},{10,11... | collective-permute-start | bytes 1572872 | tf_op jit(solution)/shard_map/ppermute | solution.py:393
  190.0 17.8 %collective-permute-start.43 = (bf16[288,1152]{1,0:T(8,128)(2,1)S(1)}, bf16[288,1152]{1,0:T(8,128)(2,1)S(1)}, u32[]{:S(2)}, u32[]{:S(2)}) collective-permute-start(bf16[288,1152]{1,0:T(8,128)(2,1)S(1)} %get-tuple-element.135.own), channel_id=1, source_target_pairs={{0,8},{8,0},{16,24},{24,16},{1,9},{9,1},{17,25},{25,17},{2,10},{10... | collective-permute-start | bytes 1990664 | tf_op jit(solution)/shard_map/ppermute | solution.py:390
  190.8 18.3 %collective-permute-start.44 = (bf16[288,1152]{1,0:T(8,128)(2,1)S(1)}, bf16[288,1152]{1,0:T(8,128)(2,1)S(1)}, u32[]{:S(2)}, u32[]{:S(2)}) collective-permute-start(bf16[288,1152]{1,0:T(8,128)(2,1)S(1)} %get-tuple-element.135.own), channel_id=1, source_target_pairs={{0,16},{8,24},{16,0},{24,8},{1,17},{9,25},{17,1},{25,9},{2,18},{10... | collective-permute-start | bytes 1990664 | tf_op jit(solution)/shard_map/ppermute | solution.py:390
  198.9 16.0 %collective-permute-start.21 = (bf16[1,144,1152]{2,1,0:T(8,128)(2,1)S(1)}, bf16[1,144,1152]{2,1,0:T(8,128)(2,1)S(1)}, u32[]{:S(2)}, u32[]{:S(2)}) collective-permute-start(bf16[1,144,1152]{2,1,0:T(8,128)(2,1)S(1)} %get-tuple-element.110), channel_id=1, source_target_pairs={{0,8},{8,0},{16,24},{24,16},{1,9},{9,1},{17,25},{25,17},{2,10},{10... | collective-permute-start | bytes 995336 | tf_op jit(solution)/shard_map/ppermute | solution.py:390
  200.4 16.0 %collective-permute-start.24 = (bf16[1,144,1152]{2,1,0:T(8,128)(2,1)S(1)}, bf16[1,144,1152]{2,1,0:T(8,128)(2,1)S(1)}, u32[]{:S(2)}, u32[]{:S(2)}) collective-permute-start(bf16[1,144,1152]{2,1,0:T(8,128)(2,1)S(1)} %get-tuple-element.112), channel_id=1, source_target_pairs={{0,16},{8,24},{16,0},{24,8},{1,17},{9,25},{17,1},{25,9},{2,18},{10... | collective-permute-start | bytes 995336 | tf_op jit(solution)/shard_map/ppermute | solution.py:390
  207.8 14.9 %collective-permute-start.23 = (bf16[1,144,1152]{2,1,0:T(8,128)(2,1)S(1)}, bf16[1,144,1152]{2,1,0:T(8,128)(2,1)S(1)}, u32[]{:S(2)}, u32[]{:S(2)}) collective-permute-start(bf16[1,144,1152]{2,1,0:T(8,128)(2,1)S(1)} %get-tuple-element.156), channel_id=1, source_target_pairs={{0,16},{8,24},{16,0},{24,8},{1,17},{9,25},{17,1},{25,9},{2,18},{10... | collective-permute-start | bytes 995336 | tf_op jit(solution)/shard_map/ppermute | solution.py:390
  209.1 13.7 %collective-permute-start.26 = (bf16[1,144,1152]{2,1,0:T(8,128)(2,1)S(1)}, bf16[1,144,1152]{2,1,0:T(8,128)(2,1)S(1)}, u32[]{:S(2)}, u32[]{:S(2)}) collective-permute-start(bf16[1,144,1152]{2,1,0:T(8,128)(2,1)S(1)} %get-tuple-element.155), channel_id=1, source_target_pairs={{0,8},{8,0},{16,24},{24,16},{1,9},{9,1},{17,25},{25,17},{2,10},{10... | collective-permute-start | bytes 995336 | tf_op jit(solution)/shard_map/ppermute | solution.py:390
  209.9 19.2 %collective-permute-start.45 = (bf16[144,1152]{1,0:T(8,128)(2,1)S(1)}, bf16[144,1152]{1,0:T(8,128)(2,1)S(1)}, u32[]{:S(2)}, u32[]{:S(2)}) collective-permute-start(bf16[144,1152]{1,0:T(8,128)(2,1)S(1)} %slice.84), channel_id=1, source_target_pairs={{0,8},{8,0},{16,24},{24,16},{1,9},{9,1},{17,25},{25,17},{2,10},{10... | collective-permute-start | bytes 995336 | tf_op jit(solution)/shard_map/ppermute | solution.py:390
  214.9 14.9 %collective-permute-start.46 = (bf16[144,1152]{1,0:T(8,128)(2,1)S(1)}, bf16[144,1152]{1,0:T(8,128)(2,1)S(1)}, u32[]{:S(2)}, u32[]{:S(2)}) collective-permute-start(bf16[144,1152]{1,0:T(8,128)(2,1)S(1)} %slice.85), channel_id=1, source_target_pairs={{0,16},{8,24},{16,0},{24,8},{1,17},{9,25},{17,1},{25,9},{2,18},{10... | collective-permute-start | bytes 995336 | tf_op jit(solution)/shard_map/ppermute | solution.py:390
  216.4 29.8 %collective-permute-start.54 = (bf16[512,512]{1,0:T(8,128)(2,1)S(1)}, bf16[512,512]{1,0:T(8,128)(2,1)S(1)}, u32[]{:S(2)}, u32[]{:S(2)}) collective-permute-start(bf16[512,512]{1,0:T(8,128)(2,1)S(1)} %add_convert_fusion.3), channel_id=1, source_target_pairs={{0,2},{1,3},{2,4},{3,5},{4,6},{5,7},{6,0},{7,1},{8,10},{9,11},{10,... | collective-permute-start | bytes 1572872 | tf_op jit(solution)/shard_map/ppermute | solution.py:396
  224.0 20.8 %collective-permute-start.39 = (bf16[288,1152]{1,0:T(8,128)(2,1)S(1)}, bf16[288,1152]{1,0:T(8,128)(2,1)S(1)}, u32[]{:S(2)}, u32[]{:S(2)}) collective-permute-start(bf16[288,1152]{1,0:T(8,128)(2,1)S(1)} %get-tuple-element.133.own), channel_id=1, source_target_pairs={{0,8},{8,0},{16,24},{24,16},{1,9},{9,1},{17,25},{25,17},{2,10},{10... | collective-permute-start | bytes 1990664 | tf_op jit(solution)/shard_map/ppermute | solution.py:390
  225.4 18.0 %collective-permute-start.40 = (bf16[288,1152]{1,0:T(8,128)(2,1)S(1)}, bf16[288,1152]{1,0:T(8,128)(2,1)S(1)}, u32[]{:S(2)}, u32[]{:S(2)}) collective-permute-start(bf16[288,1152]{1,0:T(8,128)(2,1)S(1)} %get-tuple-element.133.own), channel_id=1, source_target_pairs={{0,16},{8,24},{16,0},{24,8},{1,17},{9,25},{17,1},{25,9},{2,18},{10... | collective-permute-start | bytes 1990664 | tf_op jit(solution)/shard_map/ppermute | solution.py:390
  240.2 6.0 %collective-permute-start.52 = (bf16[512,512]{1,0:T(8,128)(2,1)S(1)}, bf16[512,512]{1,0:T(8,128)(2,1)S(1)}, u32[]{:S(2)}, u32[]{:S(2)}) collective-permute-start(bf16[512,512]{1,0:T(8,128)(2,1)S(1)} %get-tuple-element.145), channel_id=1, source_target_pairs={{0,1},{1,0},{2,3},{3,2},{4,5},{5,4},{6,7},{7,6},{8,9},{9,8},{10,11... | collective-permute-start | bytes 1572872 | tf_op jit(solution)/shard_map/ppermute | solution.py:393
  243.4 9.2 %collective-permute-start.41 = (bf16[144,1152]{1,0:T(8,128)(2,1)S(1)}, bf16[144,1152]{1,0:T(8,128)(2,1)S(1)}, u32[]{:S(2)}, u32[]{:S(2)}) collective-permute-start(bf16[144,1152]{1,0:T(8,128)(2,1)S(1)} %slice.82), channel_id=1, source_target_pairs={{0,8},{8,0},{16,24},{24,16},{1,9},{9,1},{17,25},{25,17},{2,10},{10... | collective-permute-start | bytes 995336 | tf_op jit(solution)/shard_map/ppermute | solution.py:390
  244.8 8.9 %collective-permute-start.42 = (bf16[144,1152]{1,0:T(8,128)(2,1)S(1)}, bf16[144,1152]{1,0:T(8,128)(2,1)S(1)}, u32[]{:S(2)}, u32[]{:S(2)}) collective-permute-start(bf16[144,1152]{1,0:T(8,128)(2,1)S(1)} %slice.83), channel_id=1, source_target_pairs={{0,16},{8,24},{16,0},{24,8},{1,17},{9,25},{17,1},{25,9},{2,18},{10... | collective-permute-start | bytes 995336 | tf_op jit(solution)/shard_map/ppermute | solution.py:390
  246.4 18.5 %collective-permute-start.55 = (bf16[512,512]{1,0:T(8,128)(2,1)S(1)}, bf16[512,512]{1,0:T(8,128)(2,1)S(1)}, u32[]{:S(2)}, u32[]{:S(2)}) collective-permute-start(bf16[512,512]{1,0:T(8,128)(2,1)S(1)} %add_convert_fusion.2), channel_id=1, source_target_pairs={{0,2},{1,3},{2,4},{3,5},{4,6},{5,7},{6,0},{7,1},{8,10},{9,11},{10,... | collective-permute-start | bytes 1572872 | tf_op jit(solution)/shard_map/ppermute | solution.py:396
  253.7 34.2 %slice-start = ((s8[4718592]{0:T(1024)(128)(4,1)}), s8[4194304]{0:T(1024)(128)(4,1)S(1)}, s32[]{:S(2)}) async-start(s8[4718592]{0:T(1024)(128)(4,1)} %bitcast.26), calls=%async_computation.1 | async-start | bytes 8388608
  253.7 34.2 %slice-start.1 = ((s8[4718592]{0:T(1024)(128)(4,1)}), s8[524288]{0:T(1024)(128)(4,1)S(1)}, s32[]{:S(2)}) async-start(s8[4718592]{0:T(1024)(128)(4,1)} %bitcast.26), calls=%async_computation.2 | async-start | bytes 1048576
  264.3 19.0 %copy-start.2 = (s32[128,8]{0,1:T(8,128)S(1)}, s32[128,8]{0,1:T(8,128)}, u32[]{:S(2)}) copy-start(s32[128,8]{0,1:T(8,128)} %param.10) | copy-start | bytes 12292
  264.3 19.0 %copy-start.3 = (s32[64]{0:T(128)S(1)}, s32[64]{0:T(128)}, u32[]{:S(2)}) copy-start(s32[64]{0:T(128)} %param.12) | copy-start | bytes 772
  264.4 1.9 collective-permute-start.51
  264.4 19.7 %collective-permute-start.14 = (bf16[512,512]{1,0:T(8,128)(2,1)S(1)}, bf16[512,512]{1,0:T(8,128)(2,1)S(1)}, u32[]{:S(2)}, u32[]{:S(2)}) collective-permute-start(bf16[512,512]{1,0:T(8,128)(2,1)S(1)} %get-tuple-element.96), channel_id=1, source_target_pairs={{0,1},{1,0},{2,3},{3,2},{4,5},{5,4},{6,7},{7,6},{8,9},{9,8},{10,11... | collective-permute-start | bytes 1572872 | tf_op jit(solution)/shard_map/ppermute | solution.py:393
  266.5 17.6 %collective-permute-start.56 = (bf16[512,512]{1,0:T(8,128)(2,1)S(1)}, bf16[512,512]{1,0:T(8,128)(2,1)S(1)}, u32[]{:S(2)}, u32[]{:S(2)}) collective-permute-start(bf16[512,512]{1,0:T(8,128)(2,1)S(1)} %add_convert_fusion.1), channel_id=1, source_target_pairs={{0,2},{1,3},{2,4},{3,5},{4,6},{5,7},{6,0},{7,1},{8,10},{9,11},{10,... | collective-permute-start | bytes 1572872 | tf_op jit(solution)/shard_map/ppermute | solution.py:396
  284.3 20.4 %collective-permute-start.57 = (bf16[128,512]{1,0:T(8,128)(2,1)S(1)}, bf16[128,512]{1,0:T(8,128)(2,1)S(1)}, u32[]{:S(2)}, u32[]{:S(2)}) collective-permute-start(bf16[128,512]{1,0:T(8,128)(2,1)S(1)} %get-tuple-element.165), channel_id=1, source_target_pairs={{0,8},{8,0},{16,24},{24,16},{1,9},{9,1},{17,25},{25,17},{2,10},{10... | collective-permute-start | bytes 393224 | tf_op jit(solution)/shard_map/ppermute | solution.py:390
  285.9 18.8 %collective-permute-start.58 = (bf16[128,512]{1,0:T(8,128)(2,1)S(1)}, bf16[128,512]{1,0:T(8,128)(2,1)S(1)}, u32[]{:S(2)}, u32[]{:S(2)}) collective-permute-start(bf16[128,512]{1,0:T(8,128)(2,1)S(1)} %get-tuple-element.164), channel_id=1, source_target_pairs={{0,16},{8,24},{16,0},{24,8},{1,17},{9,25},{17,1},{25,9},{2,18},{10... | collective-permute-start | bytes 393224 | tf_op jit(solution)/shard_map/ppermute | solution.py:390
  286.6 18.1 %collective-permute-start.59 = (bf16[128,512]{1,0:T(8,128)(2,1)S(1)}, bf16[128,512]{1,0:T(8,128)(2,1)S(1)}, u32[]{:S(2)}, u32[]{:S(2)}) collective-permute-start(bf16[128,512]{1,0:T(8,128)(2,1)S(1)} %get-tuple-element.163), channel_id=1, source_target_pairs={{0,24},{8,16},{16,8},{24,0},{1,25},{9,17},{17,9},{25,1},{2,26},{10... | collective-permute-start | bytes 393224 | tf_op jit(solution)/shard_map/ppermute | solution.py:390
  (2 other events, 2.1 us)
